TPU v7x, 256 devices: a whole 4x4x8 slice. The times are simulated.
256 devices in a mesh: row: 8 (over z_hi, y), col: 32 (over z_lo, x, core).
Axes of the slice: x: 4, y: 4, z: 8 (z_hi: 2, z_lo: 4; z = z_hi * 4 + z_lo), core: 2. Of those that a mesh axis runs over, the one named last changes fastest.
Arguments:
- amplitudes: bfloat16 [4096, 512], P(('row', 'col')), may hold values from -6 to 6
- energies: float32 [4096, 512], P(('row', 'col')), may hold values from 0.5 to 4
- kernels: bfloat16 [6, 512, 512], replicated, may hold values from -0.25 to 0.25
- coefficients: bfloat16 [8, 32, 6, 1024, 512], P('row', 'col'), may hold values from -0.59765625 to 0.59765625
- target_block: int32 [8, 32, 6, 1024], P('row', 'col'), may hold values from 0 to 127
- source_block: int32 [8, 32, 6, 1024], P('row', 'col'), may hold values from 0 to 511
- slot_count: int32 [8, 32, 6], P('row', 'col'), may hold values from 204 to 1024, as said below
Outputs:
- product: float32 [4096, 512], P(('row', 'col'))
Inputs may be any that keep to these rules, and one draw needn't show every extreme that they name: `slot_count`: in every draw some tile's list for some kernel is full, with 1024 used slots; the others hold between 204 and 1024.
All inputs are finite; a program needn't handle non-finite values.
Results may differ from a plain program's by a relative error of at most 0.0004.
Values may be sent and summed in bfloat16 or wider, within the bound.
A program may use at most 128 MiB of HBM per device.

v0:
```python
import jax
import jax.numpy as jnp
from jax import lax
from jax.sharding import PartitionSpec as P


def shards(amplitudes, energies, kernels, coefficients, target_block, source_block, slot_count):
    pieces = amplitudes.shape[0]
    states = amplitudes.shape[1]
    rows_count = lax.axis_size("row")
    cols_count = lax.axis_size("col")
    row_segment = lax.all_gather(amplitudes, "col", axis=0, tiled=True)
    col_segment = lax.all_gather(amplitudes, "row", axis=0, tiled=True)
    coef_tile = coefficients[0, 0]
    target_tile = target_block[0, 0]
    source_tile = source_block[0, 0]
    count_tile = slot_count[0, 0]
    capacity = coef_tile.shape[1]
    col_blocks = rows_count * pieces
    slots = jnp.arange(capacity, dtype=jnp.int32)
    col_part = jnp.zeros((col_blocks, states), jnp.float32)
    row_part = jnp.zeros((cols_count * pieces, states), jnp.float32)
    for kernel_id in range(kernels.shape[0]):
        in_use = (slots < count_tile[kernel_id]).astype(jnp.float32)
        weight = coef_tile[kernel_id].astype(jnp.float32) * in_use[:, None]
        local_target = target_tile[kernel_id]
        local_source = source_tile[kernel_id]
        picked = row_segment[local_source]
        scaled = picked.astype(jnp.float32) * weight
        wide_kernel = kernels[kernel_id].astype(jnp.float32)
        forward = jnp.dot(scaled, wide_kernel, precision=lax.Precision.HIGHEST)
        col_part = col_part.at[local_target].add(forward)
        table = lax.dot_general(
            col_segment,
            kernels[kernel_id],
            (((1,), (1,)), ((), ())),
            preferred_element_type=jnp.float32,
        )
        row_part = row_part.at[local_source].add(table[local_target] * weight)
    diagonal_term = energies * amplitudes.astype(jnp.float32)
    column_total = lax.psum_scatter(col_part, "row", scatter_dimension=0, tiled=True)
    row_total = lax.psum_scatter(row_part, "col", scatter_dimension=0, tiled=True)
    return diagonal_term + column_total + row_total


def solution(mesh):
    in_specs = (
        P(("row", "col"), None),
        P(("row", "col"), None),
        P(),
        P("row", "col", None, None, None),
        P("row", "col", None, None),
        P("row", "col", None, None),
        P("row", "col", None),
    )
    out_specs = P(("row", "col"), None)
    return jax.shard_map(shards, mesh=mesh, in_specs=in_specs, out_specs=out_specs, check_vma=False)
```

profile of v0, /device:TPU:8, one launch (start us, length us, event | category | flops | bytes accessed | tf_op | source)
XLA Modules:
  0.0 456.3 jit_solution(16193076650276961966)
XLA Ops:
  6.5 0.8 compare_select_fusion
  7.3 0.0 copy-start.25
  7.4 46.0 %all_gather.6 = bf16[512,512]{1,0:T(8,128)(2,1)S(1)} all-gather(bf16[16,512]{1,0:T(8,128)(2,1)} %param.7), channel_id=1, replica_groups=mesh['row'=8,'col'=32] {'col'}, dimensions={0}, use_global_device_ids=true | all-gather | bytes 540672 | tf_op jit(solution)/shard_map/all_gather | solution.py:12
  53.4 1.5 fusion.129
  55.0 0.7 fusion.117
  55.7 0.8 compare_select_fusion.1
  56.5 0.0 copy-start.11
  56.5 0.0 copy-start.10
  56.5 0.0 copy-done.25
  56.5 5.1 %gather_fusion = bf16[1024,512]{1,0:T(8,128)(2,1)} fusion(bf16[512,512]{1,0:T(8,128)(2,1)S(1)} %all_gather.6, s32[1024]{0:T(1024)S(1)} %broadcast_clamp_fusion.11), kind=kCustom, calls=%fused_computation | custom fusion | bytes 2101248 | tf_op jit(solution)/shard_map/gather | solution.py:28
  61.6 5.1 %gather_fusion.1 = bf16[1024,512]{1,0:T(8,128)(2,1)} fusion(bf16[512,512]{1,0:T(8,128)(2,1)S(1)} %all_gather.6, s32[1024]{0:T(1024)S(1)} %broadcast_clamp_fusion.10), kind=kCustom, calls=%fused_computation.1 | custom fusion | bytes 2101248 | tf_op jit(solution)/shard_map/gather | solution.py:28
  66.7 0.6 fusion.118
  67.3 5.1 %gather_fusion.2 = bf16[1024,512]{1,0:T(8,128)(2,1)} fusion(bf16[512,512]{1,0:T(8,128)(2,1)S(1)} %all_gather.6, s32[1024]{0:T(1024)S(1)} %broadcast_clamp_fusion.9), kind=kCustom, calls=%fused_computation.2 | custom fusion | bytes 2101248 | tf_op jit(solution)/shard_map/gather | solution.py:28
  72.3 0.5 fusion.119
  72.9 5.1 %gather_fusion.3 = bf16[1024,512]{1,0:T(8,128)(2,1)} fusion(bf16[512,512]{1,0:T(8,128)(2,1)S(1)} %all_gather.6, s32[1024]{0:T(1024)S(1)} %broadcast_clamp_fusion.8), kind=kCustom, calls=%fused_computation.3 | custom fusion | bytes 2101248 | tf_op jit(solution)/shard_map/gather | solution.py:28
  78.0 0.6 fusion.120
  78.7 5.1 %gather_fusion.4 = bf16[1024,512]{1,0:T(8,128)(2,1)} fusion(bf16[512,512]{1,0:T(8,128)(2,1)S(1)} %all_gather.6, s32[1024]{0:T(1024)S(1)} %broadcast_clamp_fusion.7), kind=kCustom, calls=%fused_computation.4 | custom fusion | bytes 2101248 | tf_op jit(solution)/shard_map/gather | solution.py:28
  83.7 0.7 fusion.121
  84.4 0.0 copy-start.15
  84.4 0.0 slice-start
  84.5 5.2 %gather_fusion.5 = bf16[1024,512]{1,0:T(8,128)(2,1)} fusion(bf16[512,512]{1,0:T(8,128)(2,1)S(1)} %all_gather.6, s32[1024]{0:T(1024)S(1)} %broadcast_clamp_fusion.6), kind=kCustom, calls=%fused_computation.5 | custom fusion | bytes 2101248 | tf_op jit(solution)/shard_map/gather | solution.py:28
  89.7 0.0 slice-start.1
  89.7 0.7 fusion.122
  90.4 5.1 %fusion.2 = f32[1024,512]{1,0:T(8,128)} fusion(bf16[1024,512]{1,0:T(8,128)(2,1)} %gather_fusion, f32[1024]{0:T(1024)S(1)} %fusion.117, bf16[1,1,6,1024,512]{4,3,2,1,0:T(8,128)(2,1)} %param.10, bf16[6,512,512]{2,1,0:T(8,128)(2,1)} %param.9), kind=kOutput, calls=%fused_computation.38 | convolution fusion | flops 3223322624 | bytes 4722688 | tf_op jit(solution)/shard_map/dot_general | solution.py:31
  95.5 5.0 %fusion.10 = f32[1024,512]{1,0:T(8,128)} fusion(bf16[1024,512]{1,0:T(8,128)(2,1)} %gather_fusion.1, f32[1024]{0:T(1024)S(1)} %fusion.118, bf16[1,1,6,1024,512]{4,3,2,1,0:T(8,128)(2,1)} %param.10, bf16[6,512,512]{2,1,0:T(8,128)(2,1)} %param.9), kind=kOutput, calls=%fused_computation.44 | convolution fusion | flops 3223322624 | bytes 4722688 | tf_op jit(solution)/shard_map/dot_general | solution.py:31
  100.6 3.3 fusion.18
  103.9 3.3 fusion.26
  107.2 3.3 fusion.34
  110.5 3.3 fusion.42
  113.8 7.5 %scatter_custom_fusion = f32[128,512]{1,0:T(8,128)S(1)} fusion(s32[1024]{0:T(1024)S(1)} %bitcast.198, f32[1024,512]{1,0:T(8,128)} %fusion.2, f32[]{:T(128)} %constant.4.clone.1), kind=kCustom, calls=%fused_computation.139 | custom fusion | flops 524288 | bytes 262656 | tf_op jit(solution)/shard_map/scatter-add | solution.py:32
  121.3 7.5 %scatter_fusion = f32[128,512]{1,0:T(8,128)S(1)} fusion(f32[128,512]{1,0:T(8,128)S(1)} %scatter_custom_fusion, s32[1024]{0:T(1024)S(1)} %bitcast.184, f32[1024,512]{1,0:T(8,128)} %fusion.10), kind=kCustom, calls=%fused_computation.13 | custom fusion | flops 524288 | bytes 6295552 | tf_op jit(solution)/shard_map/scatter-add | solution.py:32
  128.9 6.7 %scatter_fusion.1 = f32[128,512]{1,0:T(8,128)S(1)} fusion(f32[128,512]{1,0:T(8,128)S(1)} %scatter_fusion, s32[1024]{0:T(1024)S(1)} %bitcast.182, f32[1024,512]{1,0:T(8,128)S(1)} %copy-done.4), kind=kCustom, calls=%fused_computation.14 | custom fusion | flops 524288 | bytes 6295552 | tf_op jit(solution)/shard_map/scatter-add | solution.py:32
  135.6 7.5 %scatter_fusion.2 = f32[128,512]{1,0:T(8,128)S(1)} fusion(f32[128,512]{1,0:T(8,128)S(1)} %scatter_fusion.1, s32[1024]{0:T(1024)S(1)} %bitcast.180, f32[1024,512]{1,0:T(8,128)} %fusion.26), kind=kCustom, calls=%fused_computation.15 | custom fusion | flops 524288 | bytes 6295552 | tf_op jit(solution)/shard_map/scatter-add | solution.py:32
  143.1 6.7 %scatter_fusion.3 = f32[128,512]{1,0:T(8,128)S(1)} fusion(f32[128,512]{1,0:T(8,128)S(1)} %scatter_fusion.2, s32[1024]{0:T(1024)S(1)} %bitcast.178, f32[1024,512]{1,0:T(8,128)S(1)} %copy-done.3), kind=kCustom, calls=%fused_computation.16 | custom fusion | flops 524288 | bytes 6295552 | tf_op jit(solution)/shard_map/scatter-add | solution.py:32
  149.9 0.0 copy-start.9
  149.9 0.0 copy-start.2
  149.9 8.0 %scatter_fusion.4 = f32[128,512]{1,0:T(8,128)S(1)} fusion(f32[128,512]{1,0:T(8,128)S(1)} %scatter_fusion.3, s32[1024]{0:T(1024)S(1)} %bitcast.176, f32[1024,512]{1,0:T(8,128)} %fusion.42), kind=kCustom, calls=%fused_computation.17 | custom fusion | flops 524288 | bytes 6295552 | tf_op jit(solution)/shard_map/scatter-add | solution.py:32
  158.0 0.7 copy-done
  158.7 0.0 reduce-scatter.3.cloned.1.call-update
  158.7 0.0 reduce-scatter.5.cloned.1.call-start
  158.7 0.6 broadcast_clamp_fusion.5
  159.3 43.2 %all_gather.7 = bf16[128,512]{1,0:T(8,128)(2,1)S(1)} all-gather(bf16[16,512]{1,0:T(8,128)(2,1)S(1)} %copy-done.9), channel_id=1, replica_groups=mesh['row'=8,'col'=32] {'row'}, dimensions={0}, use_global_device_ids=true | all-gather | bytes 147456 | tf_op jit(solution)/shard_map/all_gather | solution.py:13
  202.5 0.6 broadcast_clamp_fusion.4
  203.1 1.0 fusion.99
  204.1 1.0 fusion.96
  205.2 0.6 broadcast_clamp_fusion.3
  205.8 1.0 fusion.93
  206.8 0.6 broadcast_clamp_fusion.2
  207.3 1.0 fusion.90
  208.4 0.3 fusion.87
  208.7 0.6 broadcast_clamp_fusion.1
  209.3 15.5 %scatter_custom_fusion.6 = f32[512,512]{1,0:T(8,128)} fusion(s32[1024]{0:T(1024)} %bitcast.197, f32[1024]{0:T(1024)} %copy-done.13, bf16[1,1,6,1024,512]{4,3,2,1,0:T(8,128)(2,1)} %param.10, f32[]{:T(128)} %constant.4.clone.1, f32[128,512]{1,0:T(8,128)} %fusion.99, s32[1024]{0:T(1024)} %broadcast_clamp_fusion.5), kind=kCustom, calls=%fused_computation.41 | custom fusion | flops 2097152 | bytes 2368000 | tf_op jit(solution)/shard_map/scatter-add | solution.py:39
  224.7 16.8 %scatter_custom_fusion.7 = f32[512,512]{1,0:T(8,128)} fusion(f32[512,512]{1,0:T(8,128)} %scatter_custom_fusion.6, s32[1024]{0:T(1024)} %bitcast.195, f32[1024]{0:T(1024)} %copy-done.18, bf16[1,1,6,1024,512]{4,3,2,1,0:T(8,128)(2,1)} %param.10, f32[128,512]{1,0:T(8,128)} %fusion.96, s32[1024]{0:T(1024)} %broadcast_clamp_fusion.4), kind=kCustom, calls=%fused_computation.47 | custom fusion | flops 2097152 | bytes 2367488 | tf_op jit(solution)/shard_map/scatter-add | solution.py:39
  241.5 16.6 %scatter_custom_fusion.8 = f32[512,512]{1,0:T(8,128)} fusion(f32[512,512]{1,0:T(8,128)} %scatter_custom_fusion.7, s32[1024]{0:T(1024)} %bitcast.193, f32[1024]{0:T(1024)} %copy-done.17, bf16[1,1,6,1024,512]{4,3,2,1,0:T(8,128)(2,1)} %param.10, f32[128,512]{1,0:T(8,128)} %fusion.93, s32[1024]{0:T(1024)} %broadcast_clamp_fusion.3), kind=kCustom, calls=%fused_computation.53 | custom fusion | flops 2097152 | bytes 2367488 | tf_op jit(solution)/shard_map/scatter-add | solution.py:39
  258.1 16.8 %scatter_custom_fusion.9 = f32[512,512]{1,0:T(8,128)} fusion(f32[512,512]{1,0:T(8,128)} %scatter_custom_fusion.8, s32[1024]{0:T(1024)} %bitcast.191, f32[1024]{0:T(1024)} %copy-done.16, bf16[1,1,6,1024,512]{4,3,2,1,0:T(8,128)(2,1)} %param.10, f32[128,512]{1,0:T(8,128)} %fusion.90, s32[1024]{0:T(1024)} %broadcast_clamp_fusion.2), kind=kCustom, calls=%fused_computation.59 | custom fusion | flops 2097152 | bytes 2367488 | tf_op jit(solution)/shard_map/scatter-add | solution.py:39
  274.9 13.7 %scatter_custom_fusion.10 = f32[512,512]{1,0:T(8,128)} fusion(f32[512,512]{1,0:T(8,128)} %scatter_custom_fusion.9, s32[1024]{0:T(1024)} %bitcast.189, f32[1024]{0:T(1024)} %copy-done.15, bf16[1,1,6,1024,512]{4,3,2,1,0:T(8,128)(2,1)} %param.10, f32[128,512]{1,0:T(8,128)S(1)} %fusion.87, s32[1024]{0:T(1024)} %broadcast_clamp_fusion.1), kind=kCustom, calls=%fused_computation.65 | custom fusion | flops 2097152 | bytes 2367488 | tf_op jit(solution)/shard_map/scatter-add | solution.py:39
  288.6 1.3 broadcast_clamp_fusion
  289.8 0.3 fusion.84
  290.1 0.0 copy-start.19
  290.2 13.9 %scatter_custom_fusion.11 = f32[512,512]{1,0:T(8,128)} fusion(f32[512,512]{1,0:T(8,128)} %scatter_custom_fusion.10, s32[1024]{0:T(1024)} %bitcast.187, f32[1024]{0:T(1024)} %copy-done.14, bf16[1,1,6,1024,512]{4,3,2,1,0:T(8,128)(2,1)} %param.10, f32[128,512]{1,0:T(8,128)S(1)} %fusion.84, s32[1024]{0:T(1024)} %broadcast_clamp_fusion), kind=kCustom, calls=%fused_computation.71 | custom fusion | flops 2097152 | bytes 2367488 | tf_op jit(solution)/shard_map/scatter-add | solution.py:39
  304.1 0.0 reduce-scatter.5.cloned.1.call-update
  304.1 0.0 reduce-scatter.3.cloned.1.call-done
  304.1 143.7 %reduce-scatter.5.cloned.1.call-done = f32[16,512]{1,0:T(8,128)} async-done(((f32[512,512]{1,0:T(8,128)}), f32[16,512]{1,0:T(8,128)}) %reduce-scatter.5.cloned.1.call-update) | async-done | bytes 32784 | tf_op jit(solution)/shard_map/reduce_scatter | solution.py:42
  447.8 1.4 add_add_fusion
  (53 shorter events, 0.1 us)
Async XLA Ops:
  6.5 297.6 %reduce-scatter.3.cloned.1.call-start = ((), (), s32[]{:S(2)}) async-start(), calls=%async_computation.2 | async-start | bytes 294912 | tf_op jit(solution)/shard_map/reduce_scatter | solution.py:41
  7.3 49.2 %copy-start.25 = (s32[1024,1]{0,1:T(1,128)}, s32[1024,1]{0,1:T(1,128)S(1)}, u32[]{:S(2)}) copy-start(s32[1024,1]{0,1:T(1,128)S(1)} %get-tuple-element.15) | copy-start | bytes 12292
  7.3 54.3 %copy-start.24 = (s32[1024,1]{0,1:T(1,128)}, s32[1024,1]{0,1:T(1,128)S(1)}, u32[]{:S(2)}) copy-start(s32[1024,1]{0,1:T(1,128)S(1)} %get-tuple-element.14) | copy-start | bytes 12292
  7.4 59.9 %copy-start.23 = (s32[1024,1]{0,1:T(1,128)}, s32[1024,1]{0,1:T(1,128)S(1)}, u32[]{:S(2)}) copy-start(s32[1024,1]{0,1:T(1,128)S(1)} %get-tuple-element.13) | copy-start | bytes 12292
  7.4 65.5 %copy-start.22 = (s32[1024,1]{0,1:T(1,128)}, s32[1024,1]{0,1:T(1,128)S(1)}, u32[]{:S(2)}) copy-start(s32[1024,1]{0,1:T(1,128)S(1)} %get-tuple-element.12) | copy-start | bytes 12292
  7.4 71.3 %copy-start.21 = (s32[1024,1]{0,1:T(1,128)}, s32[1024,1]{0,1:T(1,128)S(1)}, u32[]{:S(2)}) copy-start(s32[1024,1]{0,1:T(1,128)S(1)} %get-tuple-element.16) | copy-start | bytes 12292
  7.4 77.0 %copy-start.20 = (s32[1024,1]{0,1:T(1,128)}, s32[1024,1]{0,1:T(1,128)S(1)}, u32[]{:S(2)}) copy-start(s32[1024,1]{0,1:T(1,128)S(1)} %get-tuple-element.11) | copy-start | bytes 12292
  55.7 34.7 %copy-start.13 = (f32[1024]{0:T(1024)}, f32[1024]{0:T(1024)S(1)}, u32[]{:S(2)}) copy-start(f32[1024]{0:T(1024)S(1)} %fusion.117) | copy-start | bytes 12292
  56.5 86.6 %copy-start.11 = (s32[1024,1]{0,1:T(1,128)}, s32[1024,1]{0,1:T(1,128)S(1)}, u32[]{:S(2)}) copy-start(s32[1024,1]{0,1:T(1,128)S(1)} %get-tuple-element.10) | copy-start | bytes 12292
  56.5 93.4 %copy-start.10 = (s32[1024,1]{0,1:T(1,128)}, s32[1024,1]{0,1:T(1,128)S(1)}, u32[]{:S(2)}) copy-start(s32[1024,1]{0,1:T(1,128)S(1)} %get-tuple-element.5) | copy-start | bytes 12292
  67.2 28.3 %copy-start.18 = (f32[1024]{0:T(1024)}, f32[1024]{0:T(1024)S(1)}, u32[]{:S(2)}) copy-start(f32[1024]{0:T(1024)S(1)} %fusion.118) | copy-start | bytes 12292
  72.9 27.7 %copy-start.17 = (f32[1024]{0:T(1024)}, f32[1024]{0:T(1024)S(1)}, u32[]{:S(2)}) copy-start(f32[1024]{0:T(1024)S(1)} %fusion.119) | copy-start | bytes 12292
  78.6 25.3 %copy-start.16 = (f32[1024]{0:T(1024)}, f32[1024]{0:T(1024)S(1)}, u32[]{:S(2)}) copy-start(f32[1024]{0:T(1024)S(1)} %fusion.120) | copy-start | bytes 12292
  84.4 22.8 %copy-start.15 = (f32[1024]{0:T(1024)}, f32[1024]{0:T(1024)S(1)}, u32[]{:S(2)}) copy-start(f32[1024]{0:T(1024)S(1)} %fusion.121) | copy-start | bytes 12292
  84.4 16.1 %slice-start = ((s8[6291456]{0:T(1024)(128)(4,1)}), s8[2097152]{0:T(1024)(128)(4,1)S(1)}, s32[]{:S(2)}) async-start(s8[6291456]{0:T(1024)(128)(4,1)} %bitcast.174), calls=%async_computation.4 | async-start | bytes 4194304
  89.7 10.9 %slice-start.1 = ((s8[6291456]{0:T(1024)(128)(4,1)}), s8[4194304]{0:T(1024)(128)(4,1)S(1)}, s32[]{:S(2)}) async-start(s8[6291456]{0:T(1024)(128)(4,1)} %bitcast.174), calls=%async_computation.5 | async-start | bytes 8388608
  90.4 20.1 %copy-start.14 = (f32[1024]{0:T(1024)}, f32[1024]{0:T(1024)S(1)}, u32[]{:S(2)}) copy-start(f32[1024]{0:T(1024)S(1)} %fusion.122) | copy-start | bytes 12292
  95.5 5.1 %copy-start.1 = (bf16[6,512,512]{2,1,0:T(8,128)(2,1)S(1)}, bf16[6,512,512]{2,1,0:T(8,128)(2,1)}, u32[]{:S(2)}) copy-start(bf16[6,512,512]{2,1,0:T(8,128)(2,1)} %param.9) | copy-start | bytes 9437188
  95.5 5.1 %copy-start.5 = (bf16[1024,512]{1,0:T(8,128)(2,1)S(1)}, bf16[1024,512]{1,0:T(8,128)(2,1)}, u32[]{:S(2)}) copy-start(bf16[1024,512]{1,0:T(8,128)(2,1)} %gather_fusion.2) | copy-start | bytes 3145732
  100.6 3.3 copy-start.6
  103.9 3.3 copy-start.7
  107.2 3.4 copy-start.8
  121.3 7.5 %copy-start.4 = (f32[1024,512]{1,0:T(8,128)S(1)}, f32[1024,512]{1,0:T(8,128)}, u32[]{:S(2)}) copy-start(f32[1024,512]{1,0:T(8,128)} %fusion.18) | copy-start | bytes 6291460
  135.6 7.5 %copy-start.3 = (f32[1024,512]{1,0:T(8,128)S(1)}, f32[1024,512]{1,0:T(8,128)}, u32[]{:S(2)}) copy-start(f32[1024,512]{1,0:T(8,128)} %fusion.34) | copy-start | bytes 6291460
  149.9 9.5 %copy-start.9 = (bf16[16,512]{1,0:T(8,128)(2,1)S(1)}, bf16[16,512]{1,0:T(8,128)(2,1)}, u32[]{:S(2)}) copy-start(bf16[16,512]{1,0:T(8,128)(2,1)} %param.7) | copy-start | bytes 49156
  149.9 53.2 %copy-start.2 = (bf16[6,512,512]{2,1,0:T(8,128)(2,1)S(1)}, bf16[6,512,512]{2,1,0:T(8,128)(2,1)}, u32[]{:S(2)}) copy-start(bf16[6,512,512]{2,1,0:T(8,128)(2,1)} %param.9) | copy-start | bytes 9437188
  158.0 0.7 copy-start
  158.7 289.1 %reduce-scatter.5.cloned.1.call-start = ((), (), s32[]{:S(2)}) async-start(), calls=%async_computation.3 | async-start | bytes 1081344 | tf_op jit(solution)/shard_map/reduce_scatter | solution.py:42
  203.1 5.6 %copy-start.12 = (s32[1024,1]{0,1:T(1,128)S(1)}, s32[1024,1]{0,1:T(1,128)}, u32[]{:S(2)}) copy-start(s32[1024,1]{0,1:T(1,128)} %copy-done.11) | copy-start | bytes 12292
  290.1 157.7 %copy-start.19 = (f32[16,512]{1,0:T(8,128)S(1)}, f32[16,512]{1,0:T(8,128)}, u32[]{:S(2)}) copy-start(f32[16,512]{1,0:T(8,128)} %param.8) | copy-start | bytes 98308
Sparse Core Ops, SparseCore 0:
  158.8 80.2 reduce-scatter.2
  304.2 143.5 reduce-scatter.4
where the time goes:
time: 460 us; the launch traced here: 456 us
  other arithmetic  148 us (32%)
  waiting for transfers between devices  144 us (31%)
  blocking collectives  89.2 us (19%)
  local copies, waits for them, and re-layouts  32.9 us (7%)
  matrix products  28 us (6%)
  between operations  14.2 us (3%)
    reduce_scatter x1, waiting for transfers between devices, shards(): lax.psum_scatter(row_part, 'col', scatter_dimension=0, tiled=True)  144 us
    scatter-add x6, other arithmetic, shards(): row_part = row_part.at[local_source].add(table[local_target] * weight)  93.2 us
    all_gather x1, blocking collectives, shards(): row_segment = lax.all_gather(amplitudes, 'col', axis=0, tiled=True)  46 us
    scatter-add x6, other arithmetic, shards(): col_part = col_part.at[local_target].add(forward)  44 us
    all_gather x1, blocking collectives, shards(): col_segment = lax.all_gather(amplitudes, 'row', axis=0, tiled=True)  43.2 us
    gather x6, local copies, waits for them, and re-layouts, shards(): picked = row_segment[local_source]  30.5 us
    dot_general x6, matrix products, shards(): forward = jnp.dot(scaled, wide_kernel, precision=lax.Precision.HIGHEST)  23.3 us
  transfers between devices with their start and end apart: 2, of which 1 were waited for; matrix products, arithmetic and copies ran while one was open for 22% of the time, Pallas kernels for 0%

commit v1 on v0

v1 whole, which is shorter than its diff:
```python
import functools
import jax
import jax.numpy as jnp
from jax import lax
from jax.experimental import pallas as pl
from jax.experimental.pallas import tpu as pltpu
from jax.sharding import PartitionSpec as P

MESH = pl.DeviceIdType.MESH


def split(x):
    hi = x.astype(jnp.bfloat16)
    lo = (x - hi.astype(jnp.float32)).astype(jnp.bfloat16)
    return hi, lo


def onehot_rows(idx_row, count):
    slots = idx_row.shape[1]
    rows = lax.broadcasted_iota(jnp.int32, (count, slots), 0)
    return jnp.where(rows == idx_row, 1.0, 0.0).astype(jnp.bfloat16)


def onehot_cols(idx_row, count):
    slots = idx_row.shape[1]
    parts = []
    for at in range(0, slots, 128):
        wide = jnp.broadcast_to(idx_row[:, at:at + 128], (128, 128)).astype(jnp.float32).T
        tiles = []
        for base in range(0, count, 128):
            lanes = lax.broadcasted_iota(jnp.int32, (128, 128), 1).astype(jnp.float32) + float(base)
            tiles.append(jnp.where(lanes == wide, 1.0, 0.0).astype(jnp.bfloat16))
        parts.append(tiles[0] if len(tiles) == 1 else jnp.concatenate(tiles, axis=1))
    return jnp.concatenate(parts, axis=0)


def body(n_row, n_col, amp, coef, kern, tgt, src, cnt, out,
         coef_v, kern_v, row_seg, col_seg, row_part, col_part, row_recv, col_recv,
         load_sem, gather_row, gather_col, reduce_row, reduce_col, sent):
    r = lax.axis_index("row")
    c = lax.axis_index("col")
    nk, cap, states = coef_v.shape
    pb = amp.shape[0]
    n_src = n_col * pb
    n_tgt = n_row * pb
    f32 = jnp.float32

    def load(k):
        return (pltpu.make_async_copy(kern.at[k], kern_v.at[k], load_sem.at[0, k]),
                pltpu.make_async_copy(coef.at[k], coef_v.at[k], load_sem.at[1, k]))

    for k in range(nk):
        for copy in load(k):
            copy.start()

    barrier = pltpu.get_barrier_semaphore()

    def col_peer(d):
        return lax.rem(c + d, n_col)

    def row_peer(d):
        return lax.rem(r + d, n_row)

    def greet_row(d, z):
        pl.semaphore_signal(barrier, inc=1, device_id={"row": row_peer(d)}, device_id_type=MESH)
        return z

    def greet_col(d, z):
        pl.semaphore_signal(barrier, inc=1, device_id={"col": col_peer(d)}, device_id_type=MESH)
        return z

    lax.fori_loop(1, n_row, greet_row, 0)
    lax.fori_loop(1, n_col, greet_col, 0)
    pl.semaphore_wait(barrier, n_row + n_col - 2)

    own_row = pltpu.make_async_copy(amp, row_seg.at[pl.ds(pl.multiple_of(c * pb, pb), pb)], gather_row)
    own_col = pltpu.make_async_copy(amp, col_seg.at[pl.ds(pl.multiple_of(r * pb, pb), pb)], gather_col)
    own_col.start()
    own_row.start()

    def send_col_amp(d, z):
        pltpu.make_async_remote_copy(
            src_ref=amp, dst_ref=col_seg.at[pl.ds(pl.multiple_of(r * pb, pb), pb)],
            send_sem=sent.at[0], recv_sem=gather_col,
            device_id={"row": row_peer(d)}, device_id_type=MESH).start()
        return z

    def send_row_amp(d, z):
        pltpu.make_async_remote_copy(
            src_ref=amp, dst_ref=row_seg.at[pl.ds(pl.multiple_of(c * pb, pb), pb)],
            send_sem=sent.at[1], recv_sem=gather_row,
            device_id={"col": col_peer(d)}, device_id_type=MESH).start()
        return z

    lax.fori_loop(1, n_row, send_col_amp, 0)
    lax.fori_loop(1, n_col, send_row_amp, 0)

    row_part[...] = jnp.zeros_like(row_part)
    col_part[...] = jnp.zeros_like(col_part)

    pltpu.make_async_copy(col_seg, col_seg, gather_col).wait()

    def transposed(k, z):
        for copy in load(k):
            copy.wait()
        table = lax.dot_general(col_seg[...], kern_v[k], (((1,), (1,)), ((), ())), preferred_element_type=f32)
        hi, lo = split(table)
        both = jnp.concatenate([hi, lo], axis=0)
        slots = lax.broadcasted_iota(jnp.int32, (1, cap), 1)
        used = slots < cnt[k]
        tgt_row = jnp.where(used, tgt[pl.ds(k, 1), :], -1)
        src_row = jnp.where(used, src[pl.ds(k, 1), :], -1)
        pick = onehot_cols(tgt_row, n_tgt)
        picked = jnp.dot(jnp.concatenate([pick, pick], axis=1), both, preferred_element_type=f32)
        val_hi, val_lo = split(picked * coef_v[k].astype(f32))
        put = onehot_rows(src_row, n_src)
        row_part[...] += (jnp.dot(put, val_hi, preferred_element_type=f32)
                          + jnp.dot(put, val_lo, preferred_element_type=f32))
        return z

    lax.fori_loop(0, nk, transposed, 0)

    pltpu.make_async_copy(
        row_part.at[pl.ds(pl.multiple_of(c * pb, pb), pb)],
        row_recv.at[pl.ds(pl.multiple_of(c * pb, pb), pb)], reduce_row).start()

    def send_row_part(d, z):
        peer = col_peer(d)
        pltpu.make_async_remote_copy(
            src_ref=row_part.at[pl.ds(pl.multiple_of(peer * pb, pb), pb)],
            dst_ref=row_recv.at[pl.ds(pl.multiple_of(c * pb, pb), pb)],
            send_sem=sent.at[2], recv_sem=reduce_row,
            device_id={"col": peer}, device_id_type=MESH).start()
        return z

    lax.fori_loop(1, n_col, send_row_part, 0)

    pltpu.make_async_copy(row_seg, row_seg, gather_row).wait()

    def forward(k, z):
        slots = lax.broadcasted_iota(jnp.int32, (1, cap), 1)
        used = slots < cnt[k]
        tgt_row = jnp.where(used, tgt[pl.ds(k, 1), :], -1)
        src_row = jnp.where(used, src[pl.ds(k, 1), :], -1)
        pick = onehot_cols(src_row, n_src)
        picked = jnp.dot(pick, row_seg[...], preferred_element_type=f32)
        val_hi, val_lo = split(picked * coef_v[k].astype(f32))
        put = onehot_rows(tgt_row, n_tgt)
        total = (jnp.dot(put, val_hi, preferred_element_type=f32)
                 + jnp.dot(put, val_lo, preferred_element_type=f32))
        hi, lo = split(total)
        col_part[...] += (jnp.dot(hi, kern_v[k], preferred_element_type=f32)
                          + jnp.dot(lo, kern_v[k], preferred_element_type=f32))
        return z

    lax.fori_loop(0, nk, forward, 0)

    pltpu.make_async_copy(
        col_part.at[pl.ds(pl.multiple_of(r * pb, pb), pb)],
        col_recv.at[pl.ds(pl.multiple_of(r * pb, pb), pb)], reduce_col).start()

    def send_col_part(d, z):
        peer = row_peer(d)
        pltpu.make_async_remote_copy(
            src_ref=col_part.at[pl.ds(pl.multiple_of(peer * pb, pb), pb)],
            dst_ref=col_recv.at[pl.ds(pl.multiple_of(r * pb, pb), pb)],
            send_sem=sent.at[3], recv_sem=reduce_col,
            device_id={"row": peer}, device_id_type=MESH).start()
        return z

    lax.fori_loop(1, n_row, send_col_part, 0)

    pltpu.make_async_copy(row_recv, row_recv, reduce_row).wait()
    total = row_recv[pl.ds(0, pb)]
    for j in range(1, n_col):
        total = total + row_recv[pl.ds(j * pb, pb)]
    pltpu.make_async_copy(col_recv, col_recv, reduce_col).wait()
    for j in range(n_row):
        total = total + col_recv[pl.ds(j * pb, pb)]
    out[...] = total

    others_row = pl.ds(0, (n_row - 1) * pb)
    others_col = pl.ds(0, (n_col - 1) * pb)
    pltpu.make_async_copy(col_seg.at[others_row], col_seg.at[others_row], sent.at[0]).wait()
    pltpu.make_async_copy(row_seg.at[others_col], row_seg.at[others_col], sent.at[1]).wait()
    pltpu.make_async_copy(row_recv.at[others_col], row_recv.at[others_col], sent.at[2]).wait()
    pltpu.make_async_copy(col_recv.at[others_row], col_recv.at[others_row], sent.at[3]).wait()


def shards(amplitudes, energies, kernels, coefficients, target_block, source_block, slot_count):
    pb, states = amplitudes.shape
    n_row = lax.axis_size("row")
    n_col = lax.axis_size("col")
    nk, cap = coefficients.shape[2:4]
    vmem = pl.BlockSpec(memory_space=pltpu.VMEM)
    hbm = pl.BlockSpec(memory_space=pl.ANY)
    dma = pltpu.SemaphoreType.DMA
    bf16, f32 = jnp.bfloat16, jnp.float32
    total = pl.pallas_call(
        functools.partial(body, n_row, n_col),
        out_shape=jax.ShapeDtypeStruct((pb, states), f32),
        in_specs=[vmem, hbm, hbm, vmem, vmem, pl.BlockSpec(memory_space=pltpu.SMEM)],
        out_specs=vmem,
        scratch_shapes=[
            pltpu.VMEM((nk, cap, states), bf16),
            pltpu.VMEM((nk, states, states), bf16),
            pltpu.VMEM((n_col * pb, states), bf16),
            pltpu.VMEM((n_row * pb, states), bf16),
            pltpu.VMEM((n_col * pb, states), f32),
            pltpu.VMEM((n_row * pb, states), f32),
            pltpu.VMEM((n_col * pb, states), f32),
            pltpu.VMEM((n_row * pb, states), f32),
            dma((2, nk)), dma, dma, dma, dma, dma((4,)),
        ],
        compiler_params=pltpu.CompilerParams(
            collective_id=0, has_side_effects=True, vmem_limit_bytes=56 * 1024 * 1024),
        name="couplings",
    )(amplitudes, coefficients[0, 0], kernels, target_block[0, 0], source_block[0, 0], slot_count[0, 0])
    return total + energies * amplitudes.astype(f32)


def solution(mesh):
    in_specs = (
        P(("row", "col"), None),
        P(("row", "col"), None),
        P(),
        P("row", "col", None, None, None),
        P("row", "col", None, None),
        P("row", "col", None, None),
        P("row", "col", None),
    )
    out_specs = P(("row", "col"), None)
    return jax.shard_map(shards, mesh=mesh, in_specs=in_specs, out_specs=out_specs, check_vma=False)
```

time: 460 us -> 61.1 us (0.13)
  the two profiles are of different devices: /device:TPU:8 before, /device:TPU:39 now
where the time goes in v1:
time: 61.1 us; the launch traced here: 60.9 us
  Pallas kernels  58 us (95%)
  local copies, waits for them, and re-layouts  1.41 us (2%)
  other arithmetic  1.38 us (2%)
    pallas_call x1, Pallas kernels, shards(): pl.pallas_call(functools.partial(body, n_row, n_col), out_shape=jax.Shape...  58 us
    unnamed x5, local copies, waits for them, and re-layouts  1.41 us
    add x1, other arithmetic, shards(): return total + energies * amplitudes.astype(f32)  1.38 us

profile of v1, /device:TPU:39, one launch (start us, length us, event | category | flops | bytes accessed | tf_op | source)
XLA Modules:
  0.0 60.9 jit_solution(12709212001482112518)
XLA Ops:
  0.0 0.0 copy-start
  0.0 0.0 copy-start.1
  0.0 1.4 %copy_bitcast_fusion = (s32[6,1024]{1,0:T(8,128)}, s32[6,1024]{1,0:T(8,128)}) fusion(s32[1,1,6,1024]{3,1,2,0:T(1,128)} %param.12, s32[1,1,6,1024]{3,1,2,0:T(1,128)} %param.11), kind=kLoop, calls=%fused_computation | loop fusion | bytes 98304
  1.4 58.0 %couplings.1 = f32[16,512]{1,0:T(8,128)} custom-call(bf16[16,512]{1,0:T(8,128)(2,1)} %amp.1, bf16[6,1024,512]{2,1,0:T(8,128)(2,1)} %bitcast.6, bf16[6,512,512]{2,1,0:T(8,128)(2,1)} %kern.1, s32[6,1024]{1,0:T(8,128)} %get-tuple-element.6.tgt, s32[6,1024]{1,0:T(8,128)} %get-tuple-element.5.src, s32[6]{0:T(128)} %bitcast.7), custom_call_target="tpu_custom_call" | custom-call | tf_op jit(solution)/shard_map/couplings/pallas_call | solution.py:199
  59.5 0.0 copy-done
  59.5 0.0 copy-done.1
  59.5 1.4 %multiply_add_fusion = f32[16,512]{1,0:T(8,128)} fusion(f32[16,512]{1,0:T(8,128)} %couplings.1, f32[16,512]{1,0:T(8,128)S(1)} %copy-done.1, bf16[16,512]{1,0:T(8,128)(2,1)S(1)} %copy-done), kind=kLoop, calls=%fused_computation.2 | loop fusion | flops 24576 | bytes 114688 | tf_op jit(solution)/shard_map/add | solution.py:219
Async XLA Ops:
  0.0 59.5 %copy-start = (bf16[16,512]{1,0:T(8,128)(2,1)S(1)}, bf16[16,512]{1,0:T(8,128)(2,1)}, u32[]{:S(2)}) copy-start(bf16[16,512]{1,0:T(8,128)(2,1)} %amp.1) | copy-start | bytes 49156
  0.0 59.5 %copy-start.1 = (f32[16,512]{1,0:T(8,128)S(1)}, f32[16,512]{1,0:T(8,128)}, u32[]{:S(2)}) copy-start(f32[16,512]{1,0:T(8,128)} %param.8) | copy-start | bytes 98308

commit v2 on v0

v2 whole, which is shorter than its diff:
```python
import functools
import jax
import jax.numpy as jnp
from jax import lax
from jax.experimental import pallas as pl
from jax.experimental.pallas import tpu as pltpu
from jax.sharding import PartitionSpec as P

MESH = pl.DeviceIdType.MESH
f32, bf16, i32, i16 = jnp.float32, jnp.bfloat16, jnp.int32, jnp.int16
LANES = 128


def split(x):
    hi = x.astype(bf16)
    return hi, (x - hi.astype(f32)).astype(bf16)


def dot(a, b):
    return jnp.dot(a, b, preferred_element_type=f32)


def encode(x):
    states = x.shape[1]
    top = jnp.maximum(jnp.max(jnp.abs(x), axis=1, keepdims=True), 1e-30)
    power = jnp.ceil(jnp.log2(jnp.broadcast_to(top, (x.shape[0], LANES)) * (1.0 / 32000.0)))
    scale = jnp.exp2(-power)
    parts = [jnp.round(x[:, at:at + LANES] * scale).astype(i32).astype(i16) for at in range(0, states, LANES)]
    return jnp.concatenate(parts + [power.astype(i32).astype(i16)], axis=1)


def decode(coded):
    states = coded.shape[1] - LANES
    scale = jnp.exp2(coded[:, states:].astype(i32).astype(f32))
    parts = [coded[:, at:at + LANES].astype(i32).astype(f32) * scale for at in range(0, states, LANES)]
    return jnp.concatenate(parts, axis=1)


def build(idx, cnt, k, rows_ref, cols_ref, count):
    one, zero = jnp.bfloat16(1), jnp.bfloat16(0)
    for m in range(idx.shape[0]):
        lane = lax.broadcasted_iota(i32, (1, LANES), 1) + m * LANES
        row = jnp.where(lane < cnt[k], idx[m:m + 1, :], -1)
        wide = jnp.broadcast_to(row, (LANES, LANES))
        down, across = wide.astype(i16), wide.T.astype(i16)
        for base in range(0, count, LANES):
            it = lax.broadcasted_iota(i16, (LANES, LANES), 0)
            rows_ref[k, pl.ds(base, LANES), pl.ds(m * LANES, LANES)] = jnp.where(it == down - jnp.int16(base), one, zero)
            it = lax.broadcasted_iota(i16, (LANES, LANES), 1)
            cols_ref[k, pl.ds(m * LANES, LANES), pl.ds(base, LANES)] = jnp.where(it == across - jnp.int16(base), one, zero)


def zip_run(*gens):
    gens = list(gens)
    while gens:
        for g in list(gens):
            try:
                next(g)
            except StopIteration:
                gens.remove(g)


def body(n_row, n_col, amp, coef, kern, tgt, src, cnt, out,
         coef_v, kern_v, row_seg, col_seg, row_part, col_part, sibling_part,
         row_code, row_land, col_code, col_land,
         t_pick, t_put, f_pick, f_put, hi_a, lo_a, hi_b, lo_b,
         load_sem, gather_row, gather_half, gather_col, cross, reduce_row, reduce_col, sent):
    r = lax.axis_index("row")
    c = lax.axis_index("col")
    core = lax.rem(c, 2)
    chip = lax.div(c, 2)
    chips = n_col // 2
    nk, cap, states = coef_v.shape
    pb = amp.shape[0]
    n_src, n_tgt = n_col * pb, n_row * pb
    half = n_src // 2
    groups = cap // LANES
    sibling = {"col": c + 1 - 2 * core}

    def piece(at):
        return pl.ds(pl.multiple_of(at * pb, pb), pb)

    def half_of(q):
        return pl.ds(pl.multiple_of(q * half, half), half)

    def load(k):
        return (pltpu.make_async_copy(kern.at[k], kern_v.at[k], load_sem.at[0, k]),
                pltpu.make_async_copy(coef.at[k], coef_v.at[k], load_sem.at[1, k]))

    def chip_peer(d):
        return lax.rem(chip + d, chips)

    def row_peer(d):
        return lax.rem(r + d, n_row)

    barrier = pltpu.get_barrier_semaphore()

    def greet_row(d, z):
        pl.semaphore_signal(barrier, inc=1, device_id={"row": row_peer(d)}, device_id_type=MESH)
        return z

    def greet_chip(d, z):
        pl.semaphore_signal(barrier, inc=1, device_id={"col": chip_peer(d) * 2 + core}, device_id_type=MESH)
        return z

    lax.fori_loop(1, n_row, greet_row, 0)
    lax.fori_loop(1, chips, greet_chip, 0)
    pl.semaphore_signal(barrier, inc=1, device_id=sibling, device_id_type=MESH)

    for k in range(nk):
        for copy in load(k):
            copy.start()
    own_row = pltpu.make_async_copy(amp, row_seg.at[piece(core * chips + chip)], gather_row)
    own_col = pltpu.make_async_copy(amp, col_seg.at[piece(r)], gather_col)
    own_col.start()
    own_row.start()

    pl.semaphore_wait(barrier, n_row + chips - 1)

    def send_col_amp(d, z):
        pltpu.make_async_remote_copy(
            src_ref=amp, dst_ref=col_seg.at[piece(r)], send_sem=sent.at[0], recv_sem=gather_col,
            device_id={"row": row_peer(d)}, device_id_type=MESH).start()
        return z

    def send_row_amp(d, z):
        pltpu.make_async_remote_copy(
            src_ref=amp, dst_ref=row_seg.at[piece(core * chips + chip)], send_sem=sent.at[1], recv_sem=gather_row,
            device_id={"col": chip_peer(d) * 2 + core}, device_id_type=MESH).start()
        return z

    lax.fori_loop(1, n_row, send_col_amp, 0)
    lax.fori_loop(1, chips, send_row_amp, 0)

    def build_both(k, z):
        at = pl.ds(pl.multiple_of(k * groups, groups), groups)
        build(tgt[at, :], cnt, k, f_put, t_pick, n_tgt)
        j = src[at, :]
        piece_of = lax.shift_right_logical(j, 4)
        spot = (piece_of & 1) * half + lax.shift_right_logical(piece_of, 1) * pb + (j & (pb - 1))
        build(spot, cnt, k, t_put, f_pick, n_src)
        return z

    lax.fori_loop(0, nk, build_both, 0)
    row_part[...] = jnp.zeros_like(row_part)
    col_part[...] = jnp.zeros_like(col_part)
    for k in range(nk):
        for copy in load(k):
            copy.wait()
    pltpu.make_async_copy(col_seg, col_seg, gather_col).wait()

    step = cap // 4

    def store_val(picked, k, at, hi, lo):
        h, l = split(picked * coef_v[k, pl.ds(at, step), :].astype(f32))
        hi[pl.ds(at, step), :] = h
        lo[pl.ds(at, step), :] = l

    def t_prep(k, hi, lo):
        table = lax.dot_general(col_seg[...], kern_v[k], (((1,), (1,)), ((), ())), preferred_element_type=f32)
        both = jnp.concatenate(split(table), axis=0)
        for at in range(0, cap, step):
            p = t_pick[k, pl.ds(at, step), :]
            store_val(dot(jnp.concatenate([p, p], axis=1), both), k, at, hi, lo)
            yield

    def t_fill(k, hi, lo):
        for at in range(0, states, 256):
            lanes = pl.ds(at, 256)
            p = t_put[k]
            row_part[:, lanes] += dot(p, hi[:, lanes]) + dot(p, lo[:, lanes])
            yield

    def f_prep(k, hi, lo):
        for at in range(0, cap, step):
            store_val(dot(f_pick[k, pl.ds(at, step), :], row_seg[...]), k, at, hi, lo)
            yield

    def f_fill(k, hi, lo):
        p = f_put[k]
        his, los = [], []
        for at in range(0, states, 256):
            lanes = pl.ds(at, 256)
            h, l = split(dot(p, hi[:, lanes]) + dot(p, lo[:, lanes]))
            his.append(h)
            los.append(l)
            yield
        h, l = jnp.concatenate(his, axis=1), jnp.concatenate(los, axis=1)
        for at in range(0, states, 256):
            lanes = pl.ds(at, 256)
            w = kern_v[k, :, lanes]
            col_part[:, lanes] += dot(h, w) + dot(l, w)
            yield

    a, b = (hi_a, lo_a), (hi_b, lo_b)
    bufs = [a, b]

    zip_run(t_prep(0, *a))
    zip_run(t_fill(0, *a), t_prep(1, *b))

    mine = half_of(core)
    pltpu.make_async_copy(row_seg.at[mine], row_seg.at[mine], gather_row).wait()
    hand = pltpu.make_async_remote_copy(
        src_ref=row_seg.at[mine], dst_ref=row_seg.at[mine], send_sem=sent.at[2], recv_sem=gather_half,
        device_id=sibling, device_id_type=MESH)
    hand.start()

    for k in range(1, nk - 1):
        zip_run(t_fill(k, *bufs[k % 2]), t_prep(k + 1, *bufs[(k + 1) % 2]))
    hand.wait()
    zip_run(t_fill(nk - 1, *bufs[(nk - 1) % 2]), f_prep(0, *bufs[nk % 2]))

    other = half_of(1 - core)
    swap = pltpu.make_async_remote_copy(
        src_ref=row_part.at[other], dst_ref=sibling_part, send_sem=sent.at[3], recv_sem=cross,
        device_id=sibling, device_id_type=MESH)
    swap.start()

    zip_run(f_fill(0, *bufs[nk % 2]), f_prep(1, *bufs[(nk + 1) % 2]))

    swap.wait()

    def code_row(i, z):
        at = pl.ds(pl.multiple_of(i * 64, 64), 64)
        total = row_part[pl.ds(pl.multiple_of(core * half + i * 64, 64), 64), :] + sibling_part[at, :]
        sibling_part[at, :] = total
        row_code[at, :] = encode(total)
        return z

    lax.fori_loop(0, half // 64, code_row, 0)

    def send_row(d, z):
        peer = chip_peer(d)
        pltpu.make_async_remote_copy(
            src_ref=row_code.at[piece(peer)], dst_ref=row_land.at[piece(chip)],
            send_sem=sent.at[4], recv_sem=reduce_row,
            device_id={"col": peer * 2 + core}, device_id_type=MESH).start()
        return z

    lax.fori_loop(1, chips, send_row, 0)
    own = pltpu.make_async_copy(row_code.at[piece(chip)], row_land.at[piece(chip)], reduce_row)
    own.start()

    for k in range(1, nk - 1):
        zip_run(f_fill(k, *bufs[(nk + k) % 2]), f_prep(k + 1, *bufs[(nk + k + 1) % 2]))
    zip_run(f_fill(nk - 1, *bufs[(2 * nk - 1) % 2]))

    col_code[...] = encode(col_part[...])

    def send_col(d, z):
        peer = row_peer(d)
        pltpu.make_async_remote_copy(
            src_ref=col_code.at[piece(peer)], dst_ref=col_land.at[piece(r)],
            send_sem=sent.at[5], recv_sem=reduce_col,
            device_id={"row": peer}, device_id_type=MESH).start()
        return z

    lax.fori_loop(1, n_row, send_col, 0)
    own = pltpu.make_async_copy(col_code.at[piece(r)], col_land.at[piece(r)], reduce_col)
    own.start()

    pltpu.make_async_copy(row_land, row_land, reduce_row).wait()
    total = decode(row_land[pl.ds(0, pb), :])
    for j in range(1, chips):
        total = total + decode(row_land[pl.ds(j * pb, pb), :])
    pltpu.make_async_copy(col_land, col_land, reduce_col).wait()
    for j in range(n_row):
        total = total + decode(col_land[pl.ds(j * pb, pb), :])
    out[...] = total

    for ref, n, sem in ((col_seg, n_row - 1, 0), (row_seg, chips - 1, 1), (row_land, chips - 1, 4), (col_land, n_row - 1, 5)):
        gone = ref.at[pl.ds(0, n * pb)]
        pltpu.make_async_copy(gone, gone, sent.at[sem]).wait()


def shards(amplitudes, energies, kernels, coefficients, target_block, source_block, slot_count):
    pb, states = amplitudes.shape
    n_row = lax.axis_size("row")
    n_col = lax.axis_size("col")
    nk, cap = coefficients.shape[2:4]
    n_src, n_tgt = n_col * pb, n_row * pb
    vmem = pl.BlockSpec(memory_space=pltpu.VMEM)
    hbm = pl.BlockSpec(memory_space=pl.ANY)
    dma = pltpu.SemaphoreType.DMA
    total = pl.pallas_call(
        functools.partial(body, n_row, n_col),
        out_shape=jax.ShapeDtypeStruct((pb, states), f32),
        in_specs=[vmem, hbm, hbm, vmem, vmem, pl.BlockSpec(memory_space=pltpu.SMEM)],
        out_specs=vmem,
        scratch_shapes=[
            pltpu.VMEM((nk, cap, states), bf16),
            pltpu.VMEM((nk, states, states), bf16),
            pltpu.VMEM((n_src, states), bf16),
            pltpu.VMEM((n_tgt, states), bf16),
            pltpu.VMEM((n_src, states), f32),
            pltpu.VMEM((n_tgt, states), f32),
            pltpu.VMEM((n_src // 2, states), f32),
            pltpu.VMEM((n_src // 2, states + LANES), i16),
            pltpu.VMEM((n_src // 2, states + LANES), i16),
            pltpu.VMEM((n_tgt, states + LANES), i16),
            pltpu.VMEM((n_tgt, states + LANES), i16),
            pltpu.VMEM((nk, cap, n_tgt), bf16),
            pltpu.VMEM((nk, n_src, cap), bf16),
            pltpu.VMEM((nk, cap, n_src), bf16),
            pltpu.VMEM((nk, n_tgt, cap), bf16),
            pltpu.VMEM((cap, states), bf16),
            pltpu.VMEM((cap, states), bf16),
            pltpu.VMEM((cap, states), bf16),
            pltpu.VMEM((cap, states), bf16),
            dma((2, nk)), dma, dma, dma, dma, dma, dma, dma((6,)),
        ],
        compiler_params=pltpu.CompilerParams(
            collective_id=0, has_side_effects=True, vmem_limit_bytes=60 * 1024 * 1024),
        name="couplings",
    )(amplitudes, coefficients.reshape(nk, cap, states), kernels,
      target_block.reshape(nk * cap // LANES, LANES), source_block.reshape(nk * cap // LANES, LANES),
      slot_count.reshape(nk))
    return total + energies * amplitudes.astype(f32)


def solution(mesh):
    in_specs = (
        P(("row", "col"), None),
        P(("row", "col"), None),
        P(),
        P("row", "col", None, None, None),
        P("row", "col", None, None),
        P("row", "col", None, None),
        P("row", "col", None),
    )
    out_specs = P(("row", "col"), None)
    return jax.shard_map(shards, mesh=mesh, in_specs=in_specs, out_specs=out_specs, check_vma=False)
```

time: 460 us -> 47 us (0.10)
  the two profiles are of different devices: /device:TPU:8 before, /device:TPU:39 now
where the time goes in v2:
time: 47 us; the launch traced here: 46.5 us
  Pallas kernels  45 us (96%)
  other arithmetic  1.38 us (3%)
    pallas_call x1, Pallas kernels, shards(): pl.pallas_call(functools.partial(body, n_row, n_col), out_shape=jax.Shape...  45 us
    add x1, other arithmetic, shards(): return total + energies * amplitudes.astype(f32)  1.38 us

profile of v2, /device:TPU:39, one launch (start us, length us, event | category | flops | bytes accessed | tf_op | source)
XLA Modules:
  0.0 46.5 jit_solution(5373685601875725232)
XLA Ops:
  0.0 0.0 copy-start
  0.0 0.0 copy-start.1
  0.0 45.0 %couplings.1 = f32[16,512]{1,0:T(8,128)} custom-call(bf16[16,512]{1,0:T(8,128)(2,1)} %amp.1, bf16[6,1024,512]{2,1,0:T(8,128)(2,1)} %bitcast.4, bf16[6,512,512]{2,1,0:T(8,128)(2,1)} %kern.1, s32[48,128]{1,0:T(8,128)} %bitcast.5, s32[48,128]{1,0:T(8,128)} %bitcast.6, s32[6]{0:T(128)} %bitcast.7), custom_call_target="tpu_custom_call" | custom-call | tf_op jit(solution)/shard_map/couplings/pallas_call | solution.py:285
  45.1 0.0 copy-done
  45.1 0.0 copy-done.1
  45.1 1.4 %multiply_add_fusion = f32[16,512]{1,0:T(8,128)} fusion(f32[16,512]{1,0:T(8,128)} %couplings.1, f32[16,512]{1,0:T(8,128)S(1)} %copy-done.1, bf16[16,512]{1,0:T(8,128)(2,1)S(1)} %copy-done), kind=kLoop, calls=%fused_computation | loop fusion | flops 24576 | bytes 114688 | tf_op jit(solution)/shard_map/add | solution.py:318
Async XLA Ops:
  0.0 45.1 %copy-start = (bf16[16,512]{1,0:T(8,128)(2,1)S(1)}, bf16[16,512]{1,0:T(8,128)(2,1)}, u32[]{:S(2)}) copy-start(bf16[16,512]{1,0:T(8,128)(2,1)} %amp.1) | copy-start | bytes 49156
  0.0 45.1 %copy-start.1 = (f32[16,512]{1,0:T(8,128)S(1)}, f32[16,512]{1,0:T(8,128)}, u32[]{:S(2)}) copy-start(f32[16,512]{1,0:T(8,128)} %param.8) | copy-start | bytes 98308

commit v3 on v2

--- a/solution.py
+++ b/solution.py
@@ -7,7 +7,7 @@
 from jax.sharding import PartitionSpec as P
 
 MESH = pl.DeviceIdType.MESH
-f32, bf16, i32, i16 = jnp.float32, jnp.bfloat16, jnp.int32, jnp.int16
+f32, bf16, i32, i16, f8 = jnp.float32, jnp.bfloat16, jnp.int32, jnp.int16, jnp.float8_e5m2
 LANES = 128
 
 
@@ -18,6 +18,12 @@
 
 def dot(a, b):
     return jnp.dot(a, b, preferred_element_type=f32)
+
+
+def level(x):
+    top = jnp.max(jnp.max(jnp.abs(x.astype(f32)), axis=0, keepdims=True), axis=1, keepdims=True)
+    top = jnp.maximum(jnp.broadcast_to(top, (1, x.shape[1])), 1e-30)
+    return jnp.ceil(jnp.log2(top * 0.125))
 
 
 def encode(x):
@@ -36,7 +42,7 @@
     return jnp.concatenate(parts, axis=1)
 
 
-def build(idx, cnt, k, rows_ref, cols_ref, count):
+def build(idx, cnt, k, rows_ref, cols_ref, count, rows8_ref=None):
     one, zero = jnp.bfloat16(1), jnp.bfloat16(0)
     for m in range(idx.shape[0]):
         lane = lax.broadcasted_iota(i32, (1, LANES), 1) + m * LANES
@@ -45,7 +51,10 @@
         down, across = wide.astype(i16), wide.T.astype(i16)
         for base in range(0, count, LANES):
             it = lax.broadcasted_iota(i16, (LANES, LANES), 0)
-            rows_ref[k, pl.ds(base, LANES), pl.ds(m * LANES, LANES)] = jnp.where(it == down - jnp.int16(base), one, zero)
+            hot = jnp.where(it == down - jnp.int16(base), one, zero)
+            rows_ref[k, pl.ds(base, LANES), pl.ds(m * LANES, LANES)] = hot
+            if rows8_ref is not None:
+                rows8_ref[k, pl.ds(base, LANES), pl.ds(m * LANES, LANES)] = hot.astype(f8)
             it = lax.broadcasted_iota(i16, (LANES, LANES), 1)
             cols_ref[k, pl.ds(m * LANES, LANES), pl.ds(base, LANES)] = jnp.where(it == across - jnp.int16(base), one, zero)
 
@@ -60,11 +69,12 @@
                 gens.remove(g)
 
 
-def body(n_row, n_col, amp, coef, kern, tgt, src, cnt, out,
+def body(n_row, n_col, amp, coef, kern, tgt_hbm, src_hbm, cnt, out,
          coef_v, kern_v, row_seg, col_seg, row_part, col_part, sibling_part,
          row_code, row_land, col_code, col_land,
-         t_pick, t_put, f_pick, f_put, hi_a, lo_a, hi_b, lo_b,
-         load_sem, gather_row, gather_half, gather_col, cross, reduce_row, reduce_col, sent):
+         t_pick, t_put, t_put8, f_pick, f_put, hi_a, lo_a, lo8_a, hi_b, lo_b, lo8_b,
+         kern_t, tab_a, tab_b, tgt, src,
+         load_sem, index_sem, gather_row, gather_half, gather_col, cross, reduce_row, reduce_col, sent):
     r = lax.axis_index("row")
     c = lax.axis_index("col")
     core = lax.rem(c, 2)
@@ -80,8 +90,7 @@
     def piece(at):
         return pl.ds(pl.multiple_of(at * pb, pb), pb)
 
-    def half_of(q):
-        return pl.ds(pl.multiple_of(q * half, half), half)
+    mine, other = pl.ds(0, half), pl.ds(half, half)
 
     def load(k):
         return (pltpu.make_async_copy(kern.at[k], kern_v.at[k], load_sem.at[0, k]),
@@ -107,10 +116,14 @@
     lax.fori_loop(1, chips, greet_chip, 0)
     pl.semaphore_signal(barrier, inc=1, device_id=sibling, device_id_type=MESH)
 
+    indices = (pltpu.make_async_copy(tgt_hbm, tgt, index_sem.at[0]),
+               pltpu.make_async_copy(src_hbm, src, index_sem.at[1]))
+    for copy in indices:
+        copy.start()
     for k in range(nk):
         for copy in load(k):
             copy.start()
-    own_row = pltpu.make_async_copy(amp, row_seg.at[piece(core * chips + chip)], gather_row)
+    own_row = pltpu.make_async_copy(amp, row_seg.at[piece(chip)], gather_row)
     own_col = pltpu.make_async_copy(amp, col_seg.at[piece(r)], gather_col)
     own_col.start()
     own_row.start()
@@ -125,20 +138,23 @@
 
     def send_row_amp(d, z):
         pltpu.make_async_remote_copy(
-            src_ref=amp, dst_ref=row_seg.at[piece(core * chips + chip)], send_sem=sent.at[1], recv_sem=gather_row,
+            src_ref=amp, dst_ref=row_seg.at[piece(chip)], send_sem=sent.at[1], recv_sem=gather_row,
             device_id={"col": chip_peer(d) * 2 + core}, device_id_type=MESH).start()
         return z
 
     lax.fori_loop(1, n_row, send_col_amp, 0)
     lax.fori_loop(1, chips, send_row_amp, 0)
+
+    for copy in indices:
+        copy.wait()
 
     def build_both(k, z):
         at = pl.ds(pl.multiple_of(k * groups, groups), groups)
         build(tgt[at, :], cnt, k, f_put, t_pick, n_tgt)
         j = src[at, :]
         piece_of = lax.shift_right_logical(j, 4)
-        spot = (piece_of & 1) * half + lax.shift_right_logical(piece_of, 1) * pb + (j & (pb - 1))
-        build(spot, cnt, k, t_put, f_pick, n_src)
+        spot = ((piece_of & 1) ^ core) * half + lax.shift_right_logical(piece_of, 1) * pb + (j & (pb - 1))
+        build(spot, cnt, k, t_put, f_pick, n_src, t_put8)
         return z
 
     lax.fori_loop(0, nk, build_both, 0)
@@ -147,83 +163,99 @@
     for k in range(nk):
         for copy in load(k):
             copy.wait()
+
+    def turn(k, z):
+        kern_t[k] = kern_v[k].T
+        return z
+
+    lax.fori_loop(0, nk, turn, 0)
     pltpu.make_async_copy(col_seg, col_seg, gather_col).wait()
 
     step = cap // 4
-
-    def store_val(picked, k, at, hi, lo):
-        h, l = split(picked * coef_v[k, pl.ds(at, step), :].astype(f32))
-        hi[pl.ds(at, step), :] = h
-        lo[pl.ds(at, step), :] = l
-
-    def t_prep(k, hi, lo):
-        table = lax.dot_general(col_seg[...], kern_v[k], (((1,), (1,)), ((), ())), preferred_element_type=f32)
-        both = jnp.concatenate(split(table), axis=0)
+    t_level = level(col_seg[...])
+    t_up, t_down = jnp.exp2(14.0 - t_level), jnp.exp2(t_level - 14.0)
+
+    def t_table(k, tab):
+        h, l = split(dot(col_seg[...], kern_t[k]))
+        tab[pl.ds(0, n_tgt), :] = h
+        tab[pl.ds(n_tgt, n_tgt), :] = l
+        yield
+
+    def t_prep(k, tab, hi, lo8):
+        both = tab[...]
         for at in range(0, cap, step):
             p = t_pick[k, pl.ds(at, step), :]
-            store_val(dot(jnp.concatenate([p, p], axis=1), both), k, at, hi, lo)
-            yield
-
-    def t_fill(k, hi, lo):
+            val = dot(jnp.concatenate([p, p], axis=1), both) * coef_v[k, pl.ds(at, step), :].astype(f32)
+            h = val.astype(bf16)
+            hi[pl.ds(at, step), :] = h
+            lo8[pl.ds(at, step), :] = ((val - h.astype(f32)) * t_up).astype(f8)
+            yield
+
+    def t_fill(k, hi, lo8, rows):
         for at in range(0, states, 256):
             lanes = pl.ds(at, 256)
-            p = t_put[k]
-            row_part[:, lanes] += dot(p, hi[:, lanes]) + dot(p, lo[:, lanes])
+            row_part[rows, lanes] += (dot(t_put[k, rows, :], hi[:, lanes])
+                                      + dot(t_put8[k, rows, :], lo8[:, lanes]) * t_down[:, at:at + 256])
             yield
 
     def f_prep(k, hi, lo):
         for at in range(0, cap, step):
-            store_val(dot(f_pick[k, pl.ds(at, step), :], row_seg[...]), k, at, hi, lo)
+            val = dot(f_pick[k, pl.ds(at, step), :], row_seg[...]) * coef_v[k, pl.ds(at, step), :].astype(f32)
+            hi[pl.ds(at, step), :], lo[pl.ds(at, step), :] = split(val)
             yield
 
     def f_fill(k, hi, lo):
         p = f_put[k]
-        his, los = [], []
+        parts = []
         for at in range(0, states, 256):
             lanes = pl.ds(at, 256)
-            h, l = split(dot(p, hi[:, lanes]) + dot(p, lo[:, lanes]))
-            his.append(h)
-            los.append(l)
-            yield
-        h, l = jnp.concatenate(his, axis=1), jnp.concatenate(los, axis=1)
+            parts.append(jnp.concatenate(split(dot(p, hi[:, lanes]) + dot(p, lo[:, lanes])), axis=0))
+            yield
+        both = jnp.concatenate(parts, axis=1)
         for at in range(0, states, 256):
             lanes = pl.ds(at, 256)
-            w = kern_v[k, :, lanes]
-            col_part[:, lanes] += dot(h, w) + dot(l, w)
-            yield
-
-    a, b = (hi_a, lo_a), (hi_b, lo_b)
-    bufs = [a, b]
-
-    zip_run(t_prep(0, *a))
-    zip_run(t_fill(0, *a), t_prep(1, *b))
-
-    mine = half_of(core)
-    pltpu.make_async_copy(row_seg.at[mine], row_seg.at[mine], gather_row).wait()
+            wide = dot(both, kern_v[k, :, lanes])
+            col_part[:, lanes] += wide[:n_tgt] + wide[n_tgt:]
+            yield
+
+    t_bufs = [(hi_a, lo8_a), (hi_b, lo8_b)]
+    bufs = [(hi_a, lo_a), (hi_b, lo_b)]
+    tabs = [tab_a, tab_b]
+    every = pl.ds(0, n_src)
     hand = pltpu.make_async_remote_copy(
-        src_ref=row_seg.at[mine], dst_ref=row_seg.at[mine], send_sem=sent.at[2], recv_sem=gather_half,
+        src_ref=row_seg.at[mine], dst_ref=row_seg.at[other], send_sem=sent.at[2], recv_sem=gather_half,
         device_id=sibling, device_id_type=MESH)
-    hand.start()
-
-    for k in range(1, nk - 1):
-        zip_run(t_fill(k, *bufs[k % 2]), t_prep(k + 1, *bufs[(k + 1) % 2]))
+
+    zip_run(t_table(0, tab_a))
+    zip_run(t_prep(0, tab_a, *t_bufs[0]), t_table(1, tab_b))
+    for k in range(nk - 1):
+        todo = [t_fill(k, *t_bufs[k % 2], every), t_prep(k + 1, tabs[(k + 1) % 2], *t_bufs[(k + 1) % 2])]
+        if k + 2 < nk:
+            todo.append(t_table(k + 2, tabs[k % 2]))
+        zip_run(*todo)
+        if k == 1:
+            pltpu.make_async_copy(row_seg.at[mine], row_seg.at[mine], gather_row).wait()
+            hand.start()
     hand.wait()
-    zip_run(t_fill(nk - 1, *bufs[(nk - 1) % 2]), f_prep(0, *bufs[nk % 2]))
-
-    other = half_of(1 - core)
+    last = t_bufs[(nk - 1) % 2]
+    first = f_prep(0, *bufs[nk % 2])
+    for done in t_fill(nk - 1, *last, other):
+        next(first)
+
     swap = pltpu.make_async_remote_copy(
         src_ref=row_part.at[other], dst_ref=sibling_part, send_sem=sent.at[3], recv_sem=cross,
         device_id=sibling, device_id_type=MESH)
     swap.start()
 
+    zip_run(t_fill(nk - 1, *last, mine), first)
+
     zip_run(f_fill(0, *bufs[nk % 2]), f_prep(1, *bufs[(nk + 1) % 2]))
 
     swap.wait()
 
     def code_row(i, z):
         at = pl.ds(pl.multiple_of(i * 64, 64), 64)
-        total = row_part[pl.ds(pl.multiple_of(core * half + i * 64, 64), 64), :] + sibling_part[at, :]
-        sibling_part[at, :] = total
+        total = row_part[at, :] + sibling_part[at, :]
         row_code[at, :] = encode(total)
         return z
 
@@ -285,7 +317,7 @@
     total = pl.pallas_call(
         functools.partial(body, n_row, n_col),
         out_shape=jax.ShapeDtypeStruct((pb, states), f32),
-        in_specs=[vmem, hbm, hbm, vmem, vmem, pl.BlockSpec(memory_space=pltpu.SMEM)],
+        in_specs=[hbm, hbm, hbm, hbm, hbm, pl.BlockSpec(memory_space=pltpu.SMEM)],
         out_specs=vmem,
         scratch_shapes=[
             pltpu.VMEM((nk, cap, states), bf16),
@@ -301,13 +333,21 @@
             pltpu.VMEM((n_tgt, states + LANES), i16),
             pltpu.VMEM((nk, cap, n_tgt), bf16),
             pltpu.VMEM((nk, n_src, cap), bf16),
+            pltpu.VMEM((nk, n_src, cap), f8),
             pltpu.VMEM((nk, cap, n_src), bf16),
             pltpu.VMEM((nk, n_tgt, cap), bf16),
             pltpu.VMEM((cap, states), bf16),
             pltpu.VMEM((cap, states), bf16),
+            pltpu.VMEM((cap, states), f8),
             pltpu.VMEM((cap, states), bf16),
             pltpu.VMEM((cap, states), bf16),
-            dma((2, nk)), dma, dma, dma, dma, dma, dma, dma((6,)),
+            pltpu.VMEM((cap, states), f8),
+            pltpu.VMEM((nk, states, states), bf16),
+            pltpu.VMEM((2 * n_tgt, states), bf16),
+            pltpu.VMEM((2 * n_tgt, states), bf16),
+            pltpu.VMEM((nk * cap // LANES, LANES), i32),
+            pltpu.VMEM((nk * cap // LANES, LANES), i32),
+            dma((2, nk)), dma((2,)), dma, dma, dma, dma, dma, dma, dma((6,)),
         ],
         compiler_params=pltpu.CompilerParams(
             collective_id=0, has_side_effects=True, vmem_limit_bytes=60 * 1024 * 1024),

time: 47 us -> 44 us (0.936)
  Pallas kernels: 45 us -> 41.9 us
    pallas_call x1, Pallas kernels: 45 us -> 41.9 us  [shards(): pl.pallas_call(functools.partial(body, n_row, n_col), out_shape=jax.Shape...]
where the time goes in v3:
time: 44 us; the launch traced here: 43.3 us
  Pallas kernels  41.9 us (95%)
  other arithmetic  1.38 us (3%)
    pallas_call x1, Pallas kernels, shards(): pl.pallas_call(functools.partial(body, n_row, n_col), out_shape=jax.Shape...  41.9 us
    add x1, other arithmetic, shards(): return total + energies * amplitudes.astype(f32)  1.38 us

profile of v3, /device:TPU:39, one launch (start us, length us, event | category | flops | bytes accessed | tf_op | source)
XLA Modules:
  0.0 43.3 jit_solution(6247271310772159197)
XLA Ops:
  0.0 0.0 copy-start
  0.0 0.0 copy-start.1
  0.0 41.9 %couplings.1 = f32[16,512]{1,0:T(8,128)} custom-call(bf16[16,512]{1,0:T(8,128)(2,1)} %amp.1, bf16[6,1024,512]{2,1,0:T(8,128)(2,1)} %bitcast.4, bf16[6,512,512]{2,1,0:T(8,128)(2,1)} %kern.1, s32[48,128]{1,0:T(8,128)} %bitcast.5, s32[48,128]{1,0:T(8,128)} %bitcast.6, s32[6]{0:T(128)} %bitcast.7), custom_call_target="tpu_custom_call" | custom-call | tf_op jit(solution)/shard_map/couplings/pallas_call | solution.py:317
  41.9 0.0 copy-done
  41.9 0.0 copy-done.1
  41.9 1.4 %multiply_add_fusion = f32[16,512]{1,0:T(8,128)} fusion(f32[16,512]{1,0:T(8,128)} %couplings.1, f32[16,512]{1,0:T(8,128)S(1)} %copy-done.1, bf16[16,512]{1,0:T(8,128)(2,1)S(1)} %copy-done), kind=kLoop, calls=%fused_computation | loop fusion | flops 24576 | bytes 114688 | tf_op jit(solution)/shard_map/add | solution.py:358
Async XLA Ops:
  0.0 41.9 %copy-start = (bf16[16,512]{1,0:T(8,128)(2,1)S(1)}, bf16[16,512]{1,0:T(8,128)(2,1)}, u32[]{:S(2)}) copy-start(bf16[16,512]{1,0:T(8,128)(2,1)} %amp.1) | copy-start | bytes 49156
  0.0 41.9 %copy-start.1 = (f32[16,512]{1,0:T(8,128)S(1)}, f32[16,512]{1,0:T(8,128)}, u32[]{:S(2)}) copy-start(f32[16,512]{1,0:T(8,128)} %param.8) | copy-start | bytes 98308

commit v4 on v3

--- a/solution.py
+++ b/solution.py
@@ -316,7 +316,7 @@
     dma = pltpu.SemaphoreType.DMA
     total = pl.pallas_call(
         functools.partial(body, n_row, n_col),
-        out_shape=jax.ShapeDtypeStruct((pb, states), f32),
+        out_shape=pltpu.VMEM((pb, states), f32),
         in_specs=[hbm, hbm, hbm, hbm, hbm, pl.BlockSpec(memory_space=pltpu.SMEM)],
         out_specs=vmem,
         scratch_shapes=[

time: 44 us -> 42.6 us (0.968)
  other arithmetic: 1.38 us -> 0.62 us
  Pallas kernels: 41.9 us -> 41.3 us
    add x1, other arithmetic: 1.38 us -> 0.62 us  [shards(): return total + energies * amplitudes.astype(f32)]
    pallas_call x1, Pallas kernels: 41.9 us -> 41.3 us  [shards(): pl.pallas_call(functools.partial(body, n_row, n_col), out_shape=pltpu.VME...]
where the time goes in v4:
time: 42.6 us; the launch traced here: 41.9 us
  Pallas kernels  41.3 us (97%)
  other arithmetic  0.62 us (1%)
    pallas_call x1, Pallas kernels, shards(): pl.pallas_call(functools.partial(body, n_row, n_col), out_shape=pltpu.VME...  41.3 us

profile of v4, /device:TPU:39, one launch (start us, length us, event | category | flops | bytes accessed | tf_op | source)
XLA Modules:
  0.0 41.9 jit_solution(2561631593991134550)
XLA Ops:
  0.0 0.0 copy-start
  0.0 0.0 copy-start.1
  0.0 41.3 %couplings.1 = f32[16,512]{1,0:T(8,128)S(1)} custom-call(bf16[16,512]{1,0:T(8,128)(2,1)} %amp.1, bf16[6,1024,512]{2,1,0:T(8,128)(2,1)} %bitcast.4, bf16[6,512,512]{2,1,0:T(8,128)(2,1)} %kern.1, s32[48,128]{1,0:T(8,128)} %bitcast.5, s32[48,128]{1,0:T(8,128)} %bitcast.6, s32[6]{0:T(128)} %bitcast.7), custom_call_target="tpu_custom_call" | custom-call | tf_op jit(solution)/shard_map/couplings/pallas_call | solution.py:317
  41.3 0.0 copy-done
  41.3 0.0 copy-done.1
  41.3 0.6 %multiply_add_fusion = f32[16,512]{1,0:T(8,128)} fusion(f32[16,512]{1,0:T(8,128)S(1)} %couplings.1, f32[16,512]{1,0:T(8,128)S(1)} %copy-done.1, bf16[16,512]{1,0:T(8,128)(2,1)S(1)} %copy-done), kind=kLoop, calls=%fused_computation | loop fusion | flops 24576 | bytes 114688 | tf_op jit(solution)/shard_map/add | solution.py:358
Async XLA Ops:
  0.0 41.3 %copy-start = (bf16[16,512]{1,0:T(8,128)(2,1)S(1)}, bf16[16,512]{1,0:T(8,128)(2,1)}, u32[]{:S(2)}) copy-start(bf16[16,512]{1,0:T(8,128)(2,1)} %amp.1) | copy-start | bytes 49156
  0.0 41.3 %copy-start.1 = (f32[16,512]{1,0:T(8,128)S(1)}, f32[16,512]{1,0:T(8,128)}, u32[]{:S(2)}) copy-start(f32[16,512]{1,0:T(8,128)} %param.8) | copy-start | bytes 98308

commit v5 on v4

--- a/solution.py
+++ b/solution.py
@@ -9,6 +9,7 @@
 MESH = pl.DeviceIdType.MESH
 f32, bf16, i32, i16, f8 = jnp.float32, jnp.bfloat16, jnp.int32, jnp.int16, jnp.float8_e5m2
 LANES = 128
+LINE = 4
 
 
 def split(x):
@@ -71,10 +72,10 @@
 
 def body(n_row, n_col, amp, coef, kern, tgt_hbm, src_hbm, cnt, out,
          coef_v, kern_v, row_seg, col_seg, row_part, col_part, sibling_part,
-         row_code, row_land, col_code, col_land,
-         t_pick, t_put, t_put8, f_pick, f_put, hi_a, lo_a, lo8_a, hi_b, lo_b, lo8_b,
+         row_code, row_land, near_code, near_land, col_code, col_land,
+         t_pick, t_put, t_put8, f_pick, f_put, t_hi, t_lo8, hi_a, lo_a, hi_b, lo_b,
          kern_t, tab_a, tab_b, tgt, src,
-         load_sem, index_sem, gather_row, gather_half, gather_col, cross, reduce_row, reduce_col, sent):
+         load_sem, index_sem, gather_row, gather_half, gather_col, cross, reduce_row, reduce_near, reduce_col, sent):
     r = lax.axis_index("row")
     c = lax.axis_index("col")
     core = lax.rem(c, 2)
@@ -83,14 +84,18 @@
     nk, cap, states = coef_v.shape
     pb = amp.shape[0]
     n_src, n_tgt = n_col * pb, n_row * pb
-    half = n_src // 2
+    lines = chips // LINE
+    line, at_x = lax.div(chip, LINE), lax.rem(chip, LINE)
+    near = 2 * LINE * pb
+    far = (chips - LINE) * pb
+    near_mine, near_other = pl.ds(0, near // 2), pl.ds(near // 2, near // 2)
+    far_mine, far_other = pl.ds(near, far), pl.ds(near + far, far)
+    near_rows = pl.ds(0, near)
     groups = cap // LANES
     sibling = {"col": c + 1 - 2 * core}
 
     def piece(at):
         return pl.ds(pl.multiple_of(at * pb, pb), pb)
-
-    mine, other = pl.ds(0, half), pl.ds(half, half)
 
     def load(k):
         return (pltpu.make_async_copy(kern.at[k], kern_v.at[k], load_sem.at[0, k]),
@@ -102,6 +107,14 @@
     def row_peer(d):
         return lax.rem(r + d, n_row)
 
+    def line_col(x, q):
+        return (line * LINE + x) * 2 + q
+
+    def far_peer(t):
+        ahead = lax.div(t, LINE) + 1
+        there = lax.rem(line + ahead, lines)
+        return (there * LINE + lax.rem(t, LINE)) * 2 + core, (lines - ahead - 1) * LINE + at_x
+
     barrier = pltpu.get_barrier_semaphore()
 
     def greet_row(d, z):
@@ -114,7 +127,12 @@
 
     lax.fori_loop(1, n_row, greet_row, 0)
     lax.fori_loop(1, chips, greet_chip, 0)
-    pl.semaphore_signal(barrier, inc=1, device_id=sibling, device_id_type=MESH)
+
+    def greet_line(x, z):
+        pl.semaphore_signal(barrier, inc=1, device_id={"col": line_col(x, 1 - core)}, device_id_type=MESH)
+        return z
+
+    lax.fori_loop(0, LINE, greet_line, 0)
 
     indices = (pltpu.make_async_copy(tgt_hbm, tgt, index_sem.at[0]),
                pltpu.make_async_copy(src_hbm, src, index_sem.at[1]))
@@ -123,12 +141,12 @@
     for k in range(nk):
         for copy in load(k):
             copy.start()
-    own_row = pltpu.make_async_copy(amp, row_seg.at[piece(chip)], gather_row)
+    own_row = pltpu.make_async_copy(amp, row_seg.at[piece(at_x)], gather_row.at[0])
     own_col = pltpu.make_async_copy(amp, col_seg.at[piece(r)], gather_col)
     own_col.start()
     own_row.start()
 
-    pl.semaphore_wait(barrier, n_row + chips - 1)
+    pl.semaphore_wait(barrier, n_row + chips + LINE - 2)
 
     def send_col_amp(d, z):
         pltpu.make_async_remote_copy(
@@ -136,14 +154,22 @@
             device_id={"row": row_peer(d)}, device_id_type=MESH).start()
         return z
 
-    def send_row_amp(d, z):
-        pltpu.make_async_remote_copy(
-            src_ref=amp, dst_ref=row_seg.at[piece(chip)], send_sem=sent.at[1], recv_sem=gather_row,
-            device_id={"col": chip_peer(d) * 2 + core}, device_id_type=MESH).start()
+    def send_near_amp(d, z):
+        pltpu.make_async_remote_copy(
+            src_ref=amp, dst_ref=row_seg.at[piece(at_x)], send_sem=sent.at[1], recv_sem=gather_row.at[0],
+            device_id={"col": line_col(lax.rem(at_x + d, LINE), core)}, device_id_type=MESH).start()
+        return z
+
+    def send_far_amp(t, z):
+        peer, spot = far_peer(t)
+        pltpu.make_async_remote_copy(
+            src_ref=amp, dst_ref=row_seg.at[piece(2 * LINE + spot)], send_sem=sent.at[1], recv_sem=gather_row.at[1],
+            device_id={"col": peer}, device_id_type=MESH).start()
         return z
 
     lax.fori_loop(1, n_row, send_col_amp, 0)
-    lax.fori_loop(1, chips, send_row_amp, 0)
+    lax.fori_loop(1, LINE, send_near_amp, 0)
+    lax.fori_loop(0, chips - LINE, send_far_amp, 0)
 
     for copy in indices:
         copy.wait()
@@ -153,7 +179,12 @@
         build(tgt[at, :], cnt, k, f_put, t_pick, n_tgt)
         j = src[at, :]
         piece_of = lax.shift_right_logical(j, 4)
-        spot = ((piece_of & 1) ^ core) * half + lax.shift_right_logical(piece_of, 1) * pb + (j & (pb - 1))
+        swapped = (piece_of & 1) ^ core
+        of_line = lax.shift_right_logical(piece_of, 1)
+        ahead = (lax.shift_right_logical(of_line, 2) - line + lines) & (lines - 1)
+        x = of_line & (LINE - 1)
+        spot = jnp.where(ahead == 0, swapped * (near // 2) + x * pb,
+                         near + swapped * far + ((ahead - 1) * LINE + x) * pb) + (j & (pb - 1))
         build(spot, cnt, k, t_put, f_pick, n_src, t_put8)
         return z
 
@@ -181,21 +212,21 @@
         tab[pl.ds(n_tgt, n_tgt), :] = l
         yield
 
-    def t_prep(k, tab, hi, lo8):
+    def t_prep(k, tab):
         both = tab[...]
         for at in range(0, cap, step):
             p = t_pick[k, pl.ds(at, step), :]
             val = dot(jnp.concatenate([p, p], axis=1), both) * coef_v[k, pl.ds(at, step), :].astype(f32)
             h = val.astype(bf16)
-            hi[pl.ds(at, step), :] = h
-            lo8[pl.ds(at, step), :] = ((val - h.astype(f32)) * t_up).astype(f8)
+            t_hi[k, pl.ds(at, step), :] = h
+            t_lo8[k, pl.ds(at, step), :] = ((val - h.astype(f32)) * t_up).astype(f8)
             yield
 
-    def t_fill(k, hi, lo8, rows):
+    def t_fill(k, rows):
         for at in range(0, states, 256):
             lanes = pl.ds(at, 256)
-            row_part[rows, lanes] += (dot(t_put[k, rows, :], hi[:, lanes])
-                                      + dot(t_put8[k, rows, :], lo8[:, lanes]) * t_down[:, at:at + 256])
+            row_part[rows, lanes] += (dot(t_put[k, rows, :], t_hi[k, :, lanes])
+                                      + dot(t_put8[k, rows, :], t_lo8[k, :, lanes]) * t_down[:, at:at + 256])
             yield
 
     def f_prep(k, hi, lo):
@@ -218,64 +249,62 @@
             col_part[:, lanes] += wide[:n_tgt] + wide[n_tgt:]
             yield
 
-    t_bufs = [(hi_a, lo8_a), (hi_b, lo8_b)]
     bufs = [(hi_a, lo_a), (hi_b, lo_b)]
     tabs = [tab_a, tab_b]
-    every = pl.ds(0, n_src)
-    hand = pltpu.make_async_remote_copy(
-        src_ref=row_seg.at[mine], dst_ref=row_seg.at[other], send_sem=sent.at[2], recv_sem=gather_half,
-        device_id=sibling, device_id_type=MESH)
+
+    def hand(n, from_rows, to_rows):
+        return pltpu.make_async_remote_copy(
+            src_ref=row_seg.at[from_rows], dst_ref=row_seg.at[to_rows], send_sem=sent.at[2 + n],
+            recv_sem=gather_half.at[n], device_id=sibling, device_id_type=MESH)
+
+    hands = (hand(0, near_mine, near_other), hand(1, far_mine, far_other))
 
     zip_run(t_table(0, tab_a))
-    zip_run(t_prep(0, tab_a, *t_bufs[0]), t_table(1, tab_b))
+    zip_run(t_prep(0, tab_a), t_table(1, tab_b))
     for k in range(nk - 1):
-        todo = [t_fill(k, *t_bufs[k % 2], every), t_prep(k + 1, tabs[(k + 1) % 2], *t_bufs[(k + 1) % 2])]
+        todo = [t_fill(k, pl.ds(near, 2 * far)), t_prep(k + 1, tabs[(k + 1) % 2])]
         if k + 2 < nk:
             todo.append(t_table(k + 2, tabs[k % 2]))
         zip_run(*todo)
         if k == 1:
-            pltpu.make_async_copy(row_seg.at[mine], row_seg.at[mine], gather_row).wait()
-            hand.start()
-    hand.wait()
-    last = t_bufs[(nk - 1) % 2]
-    first = f_prep(0, *bufs[nk % 2])
-    for done in t_fill(nk - 1, *last, other):
+            pltpu.make_async_copy(row_seg.at[near_mine], row_seg.at[near_mine], gather_row.at[0]).wait()
+            pltpu.make_async_copy(row_seg.at[far_mine], row_seg.at[far_mine], gather_row.at[1]).wait()
+            for copy in hands:
+                copy.start()
+    for copy in hands:
+        copy.wait()
+    first = f_prep(0, *bufs[0])
+    for done in t_fill(nk - 1, far_other):
         next(first)
 
     swap = pltpu.make_async_remote_copy(
-        src_ref=row_part.at[other], dst_ref=sibling_part, send_sem=sent.at[3], recv_sem=cross,
+        src_ref=row_part.at[far_other], dst_ref=sibling_part, send_sem=sent.at[4], recv_sem=cross,
         device_id=sibling, device_id_type=MESH)
     swap.start()
-
-    zip_run(t_fill(nk - 1, *last, mine), first)
-
-    zip_run(f_fill(0, *bufs[nk % 2]), f_prep(1, *bufs[(nk + 1) % 2]))
-
+    zip_run(t_fill(nk - 1, far_mine), first)
+
+    zip_run(f_fill(0, *bufs[0]), f_prep(1, *bufs[1]))
     swap.wait()
 
     def code_row(i, z):
         at = pl.ds(pl.multiple_of(i * 64, 64), 64)
-        total = row_part[at, :] + sibling_part[at, :]
-        row_code[at, :] = encode(total)
-        return z
-
-    lax.fori_loop(0, half // 64, code_row, 0)
-
-    def send_row(d, z):
-        peer = chip_peer(d)
-        pltpu.make_async_remote_copy(
-            src_ref=row_code.at[piece(peer)], dst_ref=row_land.at[piece(chip)],
-            send_sem=sent.at[4], recv_sem=reduce_row,
-            device_id={"col": peer * 2 + core}, device_id_type=MESH).start()
-        return z
-
-    lax.fori_loop(1, chips, send_row, 0)
-    own = pltpu.make_async_copy(row_code.at[piece(chip)], row_land.at[piece(chip)], reduce_row)
-    own.start()
+        row_code[at, :] = encode(row_part[pl.ds(pl.multiple_of(near + i * 64, 64), 64), :] + sibling_part[at, :])
+        return z
+
+    lax.fori_loop(0, far // 64, code_row, 0)
+
+    def send_row(t, z):
+        peer, spot = far_peer(t)
+        pltpu.make_async_remote_copy(
+            src_ref=row_code.at[piece(t)], dst_ref=row_land.at[piece(spot)],
+            send_sem=sent.at[5], recv_sem=reduce_row, device_id={"col": peer}, device_id_type=MESH).start()
+        return z
+
+    lax.fori_loop(0, chips - LINE, send_row, 0)
 
     for k in range(1, nk - 1):
-        zip_run(f_fill(k, *bufs[(nk + k) % 2]), f_prep(k + 1, *bufs[(nk + k + 1) % 2]))
-    zip_run(f_fill(nk - 1, *bufs[(2 * nk - 1) % 2]))
+        zip_run(f_fill(k, *bufs[k % 2]), f_prep(k + 1, *bufs[(k + 1) % 2]))
+    zip_run(f_fill(nk - 1, *bufs[(nk - 1) % 2]))
 
     col_code[...] = encode(col_part[...])
 
@@ -283,7 +312,7 @@
         peer = row_peer(d)
         pltpu.make_async_remote_copy(
             src_ref=col_code.at[piece(peer)], dst_ref=col_land.at[piece(r)],
-            send_sem=sent.at[5], recv_sem=reduce_col,
+            send_sem=sent.at[6], recv_sem=reduce_col,
             device_id={"row": peer}, device_id_type=MESH).start()
         return z
 
@@ -291,16 +320,41 @@
     own = pltpu.make_async_copy(col_code.at[piece(r)], col_land.at[piece(r)], reduce_col)
     own.start()
 
+    for k in range(nk):
+        zip_run(t_fill(k, near_rows))
+    near_code[...] = encode(row_part[near_rows, :])
+
+    def send_near(d, z):
+        x = lax.rem(at_x + d, LINE)
+        pltpu.make_async_remote_copy(
+            src_ref=near_code.at[piece(x)], dst_ref=near_land.at[piece(at_x)],
+            send_sem=sent.at[7], recv_sem=reduce_near, device_id={"col": line_col(x, core)}, device_id_type=MESH).start()
+        return z
+
+    def send_near_across(x, z):
+        pltpu.make_async_remote_copy(
+            src_ref=near_code.at[piece(LINE + x)], dst_ref=near_land.at[piece(LINE + at_x)],
+            send_sem=sent.at[7], recv_sem=reduce_near, device_id={"col": line_col(x, 1 - core)}, device_id_type=MESH).start()
+        return z
+
+    lax.fori_loop(1, LINE, send_near, 0)
+    lax.fori_loop(0, LINE, send_near_across, 0)
+    pltpu.make_async_copy(near_code.at[piece(at_x)], near_land.at[piece(at_x)], reduce_near).start()
+
     pltpu.make_async_copy(row_land, row_land, reduce_row).wait()
     total = decode(row_land[pl.ds(0, pb), :])
-    for j in range(1, chips):
+    for j in range(1, chips - LINE):
         total = total + decode(row_land[pl.ds(j * pb, pb), :])
     pltpu.make_async_copy(col_land, col_land, reduce_col).wait()
     for j in range(n_row):
         total = total + decode(col_land[pl.ds(j * pb, pb), :])
+    pltpu.make_async_copy(near_land, near_land, reduce_near).wait()
+    for j in range(2 * LINE):
+        total = total + decode(near_land[pl.ds(j * pb, pb), :])
     out[...] = total
 
-    for ref, n, sem in ((col_seg, n_row - 1, 0), (row_seg, chips - 1, 1), (row_land, chips - 1, 4), (col_land, n_row - 1, 5)):
+    for ref, n, sem in ((col_seg, n_row - 1, 0), (row_seg, chips - 1, 1), (row_land, chips - LINE, 5),
+                        (col_land, n_row - 1, 6), (near_land, 2 * LINE - 1, 7)):
         gone = ref.at[pl.ds(0, n * pb)]
         pltpu.make_async_copy(gone, gone, sent.at[sem]).wait()
 
@@ -311,6 +365,7 @@
     n_col = lax.axis_size("col")
     nk, cap = coefficients.shape[2:4]
     n_src, n_tgt = n_col * pb, n_row * pb
+    n_far = n_src // 2 - LINE * pb
     vmem = pl.BlockSpec(memory_space=pltpu.VMEM)
     hbm = pl.BlockSpec(memory_space=pl.ANY)
     dma = pltpu.SemaphoreType.DMA
@@ -326,9 +381,11 @@
             pltpu.VMEM((n_tgt, states), bf16),
             pltpu.VMEM((n_src, states), f32),
             pltpu.VMEM((n_tgt, states), f32),
-            pltpu.VMEM((n_src // 2, states), f32),
-            pltpu.VMEM((n_src // 2, states + LANES), i16),
-            pltpu.VMEM((n_src // 2, states + LANES), i16),
+            pltpu.VMEM((n_far, states), f32),
+            pltpu.VMEM((n_far, states + LANES), i16),
+            pltpu.VMEM((n_far, states + LANES), i16),
+            pltpu.VMEM((n_src - 2 * n_far, states + LANES), i16),
+            pltpu.VMEM((n_src - 2 * n_far, states + LANES), i16),
             pltpu.VMEM((n_tgt, states + LANES), i16),
             pltpu.VMEM((n_tgt, states + LANES), i16),
             pltpu.VMEM((nk, cap, n_tgt), bf16),
@@ -336,18 +393,18 @@
             pltpu.VMEM((nk, n_src, cap), f8),
             pltpu.VMEM((nk, cap, n_src), bf16),
             pltpu.VMEM((nk, n_tgt, cap), bf16),
+            pltpu.VMEM((nk, cap, states), bf16),
+            pltpu.VMEM((nk, cap, states), f8),
             pltpu.VMEM((cap, states), bf16),
             pltpu.VMEM((cap, states), bf16),
-            pltpu.VMEM((cap, states), f8),
             pltpu.VMEM((cap, states), bf16),
             pltpu.VMEM((cap, states), bf16),
-            pltpu.VMEM((cap, states), f8),
             pltpu.VMEM((nk, states, states), bf16),
             pltpu.VMEM((2 * n_tgt, states), bf16),
             pltpu.VMEM((2 * n_tgt, states), bf16),
             pltpu.VMEM((nk * cap // LANES, LANES), i32),
             pltpu.VMEM((nk * cap // LANES, LANES), i32),
-            dma((2, nk)), dma((2,)), dma, dma, dma, dma, dma, dma, dma((6,)),
+            dma((2, nk)), dma((2,)), dma((2,)), dma((2,)), dma, dma, dma, dma, dma, dma((8,)),
         ],
         compiler_params=pltpu.CompilerParams(
             collective_id=0, has_side_effects=True, vmem_limit_bytes=60 * 1024 * 1024),

time: 42.6 us -> 41.6 us (0.977)
  Pallas kernels: 41.3 us -> 40.4 us
    pallas_call x1, Pallas kernels: 41.3 us -> 40.4 us  [shards(): pl.pallas_call(functools.partial(body, n_row, n_col), out_shape=pltpu.VME...]
where the time goes in v5:
time: 41.6 us; the launch traced here: 41.1 us
  Pallas kernels  40.4 us (97%)
  other arithmetic  0.62 us (1%)
    pallas_call x1, Pallas kernels, shards(): pl.pallas_call(functools.partial(body, n_row, n_col), out_shape=pltpu.VME...  40.4 us

profile of v5, /device:TPU:39, one launch (start us, length us, event | category | flops | bytes accessed | tf_op | source)
XLA Modules:
  0.0 41.1 jit_solution(11995386014314614084)
XLA Ops:
  0.0 0.0 copy-start
  0.0 0.0 copy-start.1
  0.0 40.4 %couplings.1 = f32[16,512]{1,0:T(8,128)S(1)} custom-call(bf16[16,512]{1,0:T(8,128)(2,1)} %amp.1, bf16[6,1024,512]{2,1,0:T(8,128)(2,1)} %bitcast.4, bf16[6,512,512]{2,1,0:T(8,128)(2,1)} %kern.1, s32[48,128]{1,0:T(8,128)} %bitcast.5, s32[48,128]{1,0:T(8,128)} %bitcast.6, s32[6]{0:T(128)} %bitcast.7), custom_call_target="tpu_custom_call" | custom-call | tf_op jit(solution)/shard_map/couplings/pallas_call | solution.py:372
  40.4 0.0 copy-done
  40.4 0.0 copy-done.1
  40.4 0.6 %multiply_add_fusion = f32[16,512]{1,0:T(8,128)} fusion(f32[16,512]{1,0:T(8,128)S(1)} %couplings.1, f32[16,512]{1,0:T(8,128)S(1)} %copy-done.1, bf16[16,512]{1,0:T(8,128)(2,1)S(1)} %copy-done), kind=kLoop, calls=%fused_computation | loop fusion | flops 24576 | bytes 114688 | tf_op jit(solution)/shard_map/add | solution.py:415
Async XLA Ops:
  0.0 40.4 %copy-start = (bf16[16,512]{1,0:T(8,128)(2,1)S(1)}, bf16[16,512]{1,0:T(8,128)(2,1)}, u32[]{:S(2)}) copy-start(bf16[16,512]{1,0:T(8,128)(2,1)} %amp.1) | copy-start | bytes 49156
  0.0 40.4 %copy-start.1 = (f32[16,512]{1,0:T(8,128)S(1)}, f32[16,512]{1,0:T(8,128)}, u32[]{:S(2)}) copy-start(f32[16,512]{1,0:T(8,128)} %param.8) | copy-start | bytes 98308

commit v6 on v5

--- a/solution.py
+++ b/solution.py
@@ -70,11 +70,11 @@
                 gens.remove(g)
 
 
-def body(n_row, n_col, amp, coef, kern, tgt_hbm, src_hbm, cnt, out,
+def body(n_row, n_col, amp, coef, kern, tgt_hbm, src_hbm, cnt_hbm, out,
          coef_v, kern_v, row_seg, col_seg, row_part, col_part, sibling_part,
          row_code, row_land, near_code, near_land, col_code, col_land,
          t_pick, t_put, t_put8, f_pick, f_put, t_hi, t_lo8, hi_a, lo_a, hi_b, lo_b,
-         kern_t, tab_a, tab_b, tgt, src,
+         kern_t, tab_a, tab_b, tgt, src, cnt,
          load_sem, index_sem, gather_row, gather_half, gather_col, cross, reduce_row, reduce_near, reduce_col, sent):
     r = lax.axis_index("row")
     c = lax.axis_index("col")
@@ -135,7 +135,8 @@
     lax.fori_loop(0, LINE, greet_line, 0)
 
     indices = (pltpu.make_async_copy(tgt_hbm, tgt, index_sem.at[0]),
-               pltpu.make_async_copy(src_hbm, src, index_sem.at[1]))
+               pltpu.make_async_copy(src_hbm, src, index_sem.at[1]),
+               pltpu.make_async_copy(cnt_hbm, cnt, index_sem.at[2]))
     for copy in indices:
         copy.start()
     for k in range(nk):
@@ -372,7 +373,7 @@
     total = pl.pallas_call(
         functools.partial(body, n_row, n_col),
         out_shape=pltpu.VMEM((pb, states), f32),
-        in_specs=[hbm, hbm, hbm, hbm, hbm, pl.BlockSpec(memory_space=pltpu.SMEM)],
+        in_specs=[hbm] * 6,
         out_specs=vmem,
         scratch_shapes=[
             pltpu.VMEM((nk, cap, states), bf16),
@@ -404,7 +405,8 @@
             pltpu.VMEM((2 * n_tgt, states), bf16),
             pltpu.VMEM((nk * cap // LANES, LANES), i32),
             pltpu.VMEM((nk * cap // LANES, LANES), i32),
-            dma((2, nk)), dma((2,)), dma((2,)), dma((2,)), dma, dma, dma, dma, dma, dma((8,)),
+            pltpu.SMEM((nk,), i32),
+            dma((2, nk)), dma((3,)), dma((2,)), dma((2,)), dma, dma, dma, dma, dma, dma((8,)),
         ],
         compiler_params=pltpu.CompilerParams(
             collective_id=0, has_side_effects=True, vmem_limit_bytes=60 * 1024 * 1024),

time: 41.6 us -> 40.7 us (0.978)
  Pallas kernels: 40.4 us -> 39.6 us
    pallas_call x1, Pallas kernels: 40.4 us -> 39.6 us  [shards(): pl.pallas_call(functools.partial(body, n_row, n_col), out_shape=pltpu.VME...]
where the time goes in v6:
time: 40.7 us; the launch traced here: 40.2 us
  Pallas kernels  39.6 us (97%)
  other arithmetic  0.62 us (2%)
    pallas_call x1, Pallas kernels, shards(): pl.pallas_call(functools.partial(body, n_row, n_col), out_shape=pltpu.VME...  39.6 us

profile of v6, /device:TPU:39, one launch (start us, length us, event | category | flops | bytes accessed | tf_op | source)
XLA Modules:
  0.0 40.2 jit_solution(8316707959534895076)
XLA Ops:
  0.0 0.0 copy-start
  0.0 0.0 copy-start.1
  0.0 39.6 %couplings.1 = f32[16,512]{1,0:T(8,128)S(1)} custom-call(bf16[16,512]{1,0:T(8,128)(2,1)} %amp.1, bf16[6,1024,512]{2,1,0:T(8,128)(2,1)} %bitcast.4, bf16[6,512,512]{2,1,0:T(8,128)(2,1)} %kern.1, s32[48,128]{1,0:T(8,128)} %bitcast.5, s32[48,128]{1,0:T(8,128)} %bitcast.6, s32[6]{0:T(128)} %bitcast.7), custom_call_target="tpu_custom_call" | custom-call | tf_op jit(solution)/shard_map/couplings/pallas_call | solution.py:373
  39.6 0.0 copy-done
  39.6 0.0 copy-done.1
  39.6 0.6 %multiply_add_fusion = f32[16,512]{1,0:T(8,128)} fusion(f32[16,512]{1,0:T(8,128)S(1)} %couplings.1, f32[16,512]{1,0:T(8,128)S(1)} %copy-done.1, bf16[16,512]{1,0:T(8,128)(2,1)S(1)} %copy-done), kind=kLoop, calls=%fused_computation | loop fusion | flops 24576 | bytes 114688 | tf_op jit(solution)/shard_map/add | solution.py:417
Async XLA Ops:
  0.0 39.6 %copy-start = (bf16[16,512]{1,0:T(8,128)(2,1)S(1)}, bf16[16,512]{1,0:T(8,128)(2,1)}, u32[]{:S(2)}) copy-start(bf16[16,512]{1,0:T(8,128)(2,1)} %amp.1) | copy-start | bytes 49156
  0.0 39.6 %copy-start.1 = (f32[16,512]{1,0:T(8,128)S(1)}, f32[16,512]{1,0:T(8,128)}, u32[]{:S(2)}) copy-start(f32[16,512]{1,0:T(8,128)} %param.8) | copy-start | bytes 98308
